TPU v7x, 32 devices: a whole 2x2x4 slice. The times are simulated.
32 devices in a mesh: event: 4 (over x, core), row: 8 (over z, y).
Axes of the slice: x: 2, y: 2, z: 4, core: 2. Of those that a mesh axis runs over, the one named last changes fastest.
Arguments:
- initial_head: float32 [4, 48, 32, 384], P('event', None, 'row'), may hold values from -6 to -1.5
- sat_conductivity: float32 [64], replicated, may hold values from 0.3 to 3
- vg_alpha: float32 [64], replicated, may hold values from 0.25 to 1
- vg_n: float32 [64], replicated, may hold values from 1.3 to 2.5
- zone_map: int32 [16, 192], P('row'), may hold values from 0 to 63, as said below
- forcing_plan: int32 [4, 2, 16], P('event', None, 'row'), may hold values from 0 to 3
- tensiometer_cells: int32 [4, 2048], P('event', 'row'), may hold values from 0 to 73727
- tensiometer_heads: float32 [4, 2048], P('event', 'row'), may hold values from -6 to -1
Outputs:
- final_head: float32 [4, 48, 32, 384], P('event', None, 'row')
- misfit: float32 [], replicated
- grad_conductivity: float32 [64], replicated
- grad_alpha: float32 [64], replicated
- grad_n: float32 [64], replicated
Inputs may be any that keep to these rules, and one draw needn't show every extreme that they name: `zone_map`: the zone of a block in block row a lies among the 16 zones from a * 2 * 2 onward, taken modulo 64. `tensiometer_cells`: tensiometer j lies in the rows j // 256 * 4 to j // 256 * 4 + 3; the entry is its offset inside that block of rows, as depth * 4 * 384 + row offset * 384 + column.
All inputs are finite; a program needn't handle non-finite values.
Results may differ from a plain program's by a relative error of at most 0.0003.
Values sent between devices are 32-bit elements; how exact they have to be, the bound alone decides.
A program may use at most 64 MiB of HBM per device.

v0:
```python
import functools

import jax
import jax.numpy as jnp
from jax import lax
from jax.experimental import pallas as pl
from jax.experimental.pallas import tpu as pltpu
from jax.sharding import PartitionSpec as P

STEPS = 2
CFL = 0.4
IRRIGATION = 0.2
WATER_RANGE = 0.35
HIGHEST = lax.Precision.HIGHEST
F32 = jnp.float32
BF16 = jnp.bfloat16
LINKS = 7


def nt_dot(a, b, precision=None):
    return lax.dot_general(
        a, b, (((1,), (1,)), ((), ())), precision=precision, preferred_element_type=F32
    )


def fold(x):
    return jnp.sum(x.reshape(x.shape[0] // 8, 8, x.shape[1]), axis=0)


def kernel(
    count,
    groups,
    events,
    x_ref,
    sat_ref,
    alpha_ref,
    n_ref,
    zone_ref,
    plan_ref,
    cells_ref,
    heads_ref,
    out_ref,
    small_ref,
    HB,
    KB,
    AB,
    IC,
    LG,
    LV,
    WW,
    RV,
    QQ,
    GB,
    LAM,
    WB,
    TM,
    PB,
    TAB,
    OH,
    NC,
    NT,
    RATE,
    ACC,
    MX,
    SUMR,
    SUME,
    link_send,
    link_recv,
    max_send,
    max_recv,
    sum_send,
    sum_recv,
    ev_send,
    ev_recv,
):
    rows, depth, width = x_ref.shape
    zp = OH.shape[1]
    zones = sat_ref.shape[1]
    pos = lax.axis_index("row")
    me_event = lax.axis_index("event")
    up, down = pos - 1, pos + 1
    has_up, has_down = pos > 0, pos < count - 1
    lower_open = has_up.astype(F32)
    upper_open = has_down.astype(F32)

    def dev(row):
        return (me_event, row)

    barrier = pltpu.get_barrier_semaphore()
    for k in range(1, count):
        pl.semaphore_signal(
            barrier, 1, device_id=dev(lax.rem(pos + k, count)), device_id_type=pl.DeviceIdType.MESH
        )
    for k in range(1, groups):
        pl.semaphore_signal(
            barrier,
            1,
            device_id=(lax.rem(me_event + k, groups), pos),
            device_id_type=pl.DeviceIdType.MESH,
        )
    pl.semaphore_wait(barrier, count - 1 + groups - 1)

    def link(number, side, src, dst):
        return pltpu.make_async_remote_copy(
            src_ref=src,
            dst_ref=dst,
            send_sem=link_send.at[number, side],
            recv_sem=link_recv.at[number, side],
            device_id=dev(up if side == 0 else down),
            device_id_type=pl.DeviceIdType.MESH,
        )

    def start_pair(number, to_up, to_down):
        @pl.when(has_up)
        def _():
            link(number, 0, *to_up).start()

        @pl.when(has_down)
        def _():
            link(number, 1, *to_down).start()

    def recv_pair(number, to_up, to_down):
        @pl.when(has_down)
        def _():
            link(number, 0, *to_up).wait_recv()

        @pl.when(has_up)
        def _():
            link(number, 1, *to_down).wait_recv()

    def sent_pair(number, to_up, to_down):
        @pl.when(has_up)
        def _():
            link(number, 0, *to_up).wait_send()

        @pl.when(has_down)
        def _():
            link(number, 1, *to_down).wait_send()

    pairs = [
        ((x_ref.at[0], HB.at[0, rows + 1]), (x_ref.at[rows - 1], HB.at[0, 0])),
        ((PB.at[1], PB.at[3]), (PB.at[2], PB.at[0])),
        ((cells_ref, NC.at[1]), (cells_ref, NC.at[0])),
        ((heads_ref, NT.at[1]), (heads_ref, NT.at[0])),
        ((AB.at[0, 1], AB.at[0, rows + 1]), (AB.at[0, rows], AB.at[0, 0])),
        ((AB.at[1, 1], AB.at[1, rows + 1]), (AB.at[1, rows], AB.at[1, 0])),
        ((GB.at[0, 1], GB.at[0, rows + 1]), (GB.at[0, rows], GB.at[0, 0])),
    ]

    def start(number):
        start_pair(number, *pairs[number])

    def recv(number):
        recv_pair(number, *pairs[number])

    start(0)
    start(2)
    start(3)

    TAB[...] = jnp.zeros_like(TAB)
    TAB[0:1, :zones] = sat_ref[...]
    TAB[1:2, :zones] = alpha_ref[...]
    TAB[2:3, :zones] = n_ref[...]
    blocks = zone_ref.shape[1]
    spread = (
        lax.broadcasted_iota(jnp.int32, (blocks, width), 1) // 2
        == lax.broadcasted_iota(jnp.int32, (blocks, width), 0)
    ).astype(F32)
    ids = jnp.dot(zone_ref[...].astype(F32), spread, preferred_element_type=F32, precision=HIGHEST)
    zone_of = lax.broadcasted_iota(jnp.int32, (zp, width), 0).astype(F32)
    for pair in range(2):
        OH[pair] = jnp.where(zone_of == ids[pair : pair + 1], 1.0, 0.0)
        PB[pair + 1] = jnp.dot(TAB[...], OH[pair], precision=HIGHEST, preferred_element_type=F32)
    start(1)

    @pl.when(jnp.logical_not(has_up))
    def _():
        HB[0, 0] = x_ref[0]
        PB[0] = PB[1]
        NC[0] = cells_ref[...]
        NT[0] = heads_ref[...]
        for step in range(STEPS):
            AB[step, 0] = jnp.zeros((depth, width), F32)
        GB[0, 0] = jnp.zeros((depth, width), F32)

    @pl.when(jnp.logical_not(has_down))
    def _():
        HB[0, rows + 1] = x_ref[rows - 1]
        PB[3] = PB[2]
        NC[1] = cells_ref[...]
        NT[1] = heads_ref[...]
        for step in range(STEPS):
            AB[step, rows + 1] = jnp.zeros((depth, width), F32)
        GB[0, rows + 1] = jnp.zeros((depth, width), F32)

    ACC[...] = jnp.zeros_like(ACC)

    column = lax.broadcasted_iota(jnp.int32, (1, width), 1)
    layer = lax.broadcasted_iota(jnp.int32, (depth, 1), 0)
    right_half = jnp.where(column < width - 1, 0.5, 0.0)
    below_half = jnp.where(layer < depth - 1, 0.5, 0.0)
    ends = jnp.where((layer == 0) | (layer == depth - 1), 1.0, 0.0)

    def left(v):
        return pltpu.roll(v, width - 1, 1)

    def right(v):
        return pltpu.roll(v, 1, 1)

    def above(v):
        return pltpu.roll(v, 1, 0)

    def below(v):
        return pltpu.roll(v, depth - 1, 0)

    def over(indices, body):
        first, stride, number = indices

        def go(j, carry):
            body(first + stride * j)
            return carry

        lax.fori_loop(0, number, go, 0)

    own = (1, 1, rows)
    inner = (2, 1, rows - 2)
    edges = (1, rows - 1, 2)
    halo = (0, rows + 1, 2)

    def params(i):
        block = PB[(i + 1) // 2]
        return block[0:1], block[1:2], block[2:3]

    def face(i):
        return jnp.where(i == 0, lower_open, jnp.where(i == rows, upper_open, 1.0))

    def forcing(step, i):
        level = jnp.where(i > 2, plan_ref[step, 1], plan_ref[step, 0]).astype(F32)
        return jnp.where(layer == 0, level * IRRIGATION, jnp.where(layer == depth - 1, -1.0, 0.0))

    def cell(step, i, head):
        sat, alpha, n = params(i)
        m = 1.0 - 1.0 / n
        x = alpha * -head
        log_x = jnp.log(x)
        power = jnp.exp((n - 1.0) * log_x)
        v = 1.0 + x * power
        log_v = jnp.log(v)
        root = jnp.exp((-0.5 * m) * log_v)
        w = power * (root * root)
        rest = 1.0 - w
        q = sat * root * rest
        KB[step, i] = q * rest
        IC[step, i] = v / ((WATER_RANGE * (n - 1.0) * alpha) * w)
        LG[step, i] = log_x
        LV[step, i] = log_v
        WW[step, i] = w
        RV[step, i] = 1.0 / v
        QQ[step, i] = q

    def flow(step, i):
        h, k = HB[step, i], KB[step, i]
        inv = IC[step, i]
        k_up = (0.5 * face(i - 1)) * (KB[step, i - 1] + k)
        k_down = (0.5 * face(i)) * (k + KB[step, i + 1])
        k_y = right_half * (k + left(k))
        k_z = below_half * (k + below(k))
        f_y = k_y * (left(h) - h)
        f_z = k_z * (1.0 + h - below(h))
        net = (
            k_down * (HB[step, i + 1] - h)
            + k_up * (HB[step, i - 1] - h)
            + (f_y - right(f_y))
            + (above(f_z) - f_z)
            + forcing(step, i) * k
        )
        total = k_up + k_down + (k_y + right(k_y)) + (k_z + above(k_z)) + ends * k
        AB[step, i] = net * inv
        rate = jnp.max((total * inv).reshape(depth // 8, 8, width), axis=0)
        RATE[step] = jnp.maximum(RATE[step], rate)

    def max_copy(step, k):
        return pltpu.make_async_remote_copy(
            src_ref=MX.at[step, pos],
            dst_ref=MX.at[step, pos],
            send_sem=max_send.at[step, k],
            recv_sem=max_recv.at[step, pos],
            device_id=dev(lax.rem(pos + k, count)),
            device_id_type=pl.DeviceIdType.MESH,
        )

    def max_got(step, k):
        src = lax.rem(pos + k, count)
        return pltpu.make_async_remote_copy(
            src_ref=MX.at[step, src],
            dst_ref=MX.at[step, src],
            send_sem=max_send.at[step, k],
            recv_sem=max_recv.at[step, src],
            device_id=dev(src),
            device_id_type=pl.DeviceIdType.MESH,
        )

    def send_rate(step):
        rate = RATE[step]
        tile = rate[:, :128]
        for start_lane in range(128, width, 128):
            tile = jnp.maximum(tile, rate[:, start_lane : start_lane + 128])
        MX[step, pos] = tile
        for k in range(1, count):
            max_copy(step, k).start()

    def step_size(step):
        for k in range(1, count):
            max_got(step, k).wait_recv()
        top = jnp.max(MX[step], axis=0)
        return CFL / jnp.max(top, keepdims=True)

    RATE[...] = jnp.zeros_like(RATE)

    def first_cell(i):
        HB[0, i] = x_ref[i - 1]
        cell(0, i, x_ref[i - 1])

    over(own, first_cell)
    over(inner, functools.partial(flow, 0))
    recv(0)
    recv(1)
    over(halo, lambda i: cell(0, i, HB[0, i]))
    over(edges, functools.partial(flow, 0))
    send_rate(0)
    start(4)

    def places(cells):
        index = cells.astype(F32)
        line = jnp.floor((index + 0.5) * (1.0 / width))
        col = index - width * line
        level = jnp.floor((line + 0.5) * (1.0 / rows))
        return level, line - rows * level, col

    def pieces(t):
        one = t.astype(BF16)
        rest = t - one.astype(F32)
        two = rest.astype(BF16)
        return one, two, (rest - two.astype(F32)).astype(BF16)

    sensors = cells_ref.shape[1]
    col_of = lax.broadcasted_iota(jnp.int32, (width, sensors), 0).astype(F32)

    def counts(cells, targets, wanted):
        level, row, col = places(cells)
        cols = jnp.where(col_of == col, 1.0, 0.0)
        cols16 = cols.astype(BF16)
        if wanted is None:
            spot = row * depth + level
            lines = rows * depth
        else:
            spot = jnp.where(row == wanted, level, -1.0)
            lines = depth
        line_of = lax.broadcasted_iota(jnp.int32, (lines, sensors), 0).astype(F32)
        hit = line_of == spot
        number = nt_dot(jnp.where(hit, 1.0, 0.0).astype(BF16), cols16)
        total = None
        for piece in pieces(targets):
            part = nt_dot(jnp.where(hit, piece.astype(F32), 0.0).astype(BF16), cols16)
            total = part if total is None else total + part
        return number, total / jnp.maximum(number, 1.0), hit, cols

    number, mean, hit, cols = counts(cells_ref[...], heads_ref[...], None)
    WB[1 : rows + 1] = number.reshape(rows, depth, width)
    TM[1 : rows + 1] = mean.reshape(rows, depth, width)
    at_sensor = jnp.dot(mean, cols, precision=HIGHEST, preferred_element_type=F32)
    own_mean = jnp.sum(jnp.where(hit, at_sensor, 0.0), axis=0, keepdims=True)
    spread_sum = jnp.sum((heads_ref[...] - own_mean) ** 2, keepdims=True)
    recv(2)
    recv(3)
    for side, wanted, place in ((0, rows - 1, 0), (1, 0, rows + 1)):
        number, mean, _, _ = counts(NC[side], NT[side], wanted)
        WB[place] = number
        TM[place] = mean

    dt0 = step_size(0)

    def next_cell(i):
        head = HB[0, i] + dt0 * AB[0, i]
        HB[1, i] = head
        cell(1, i, head)

    over(own, next_cell)
    over(inner, functools.partial(flow, 1))
    recv(4)
    over(halo, next_cell)
    over(edges, functools.partial(flow, 1))
    send_rate(1)
    start(5)
    dt1 = step_size(1)
    scale = 1.0 / events

    def last_head(i):
        head = HB[1, i] + dt1 * AB[1, i]
        off = head - TM[i]
        pull = (scale * WB[i]) * off
        GB[1, i] = pull * dt1 * IC[1, i]
        return head, off * pull, pull

    def finish(i):
        head, square, pull = last_head(i)
        out_ref[i - 1] = head
        LAM[1, i] = pull
        ACC[2, 0] += fold(square)

    over(own, finish)
    recv(5)
    over(halo, lambda i: (last_head(i), None)[1])

    def pull_back(step, dt, i):
        sat, alpha, n = params(i)
        h, k, g, lam = HB[step, i], KB[step, i], GB[step, i], LAM[step, i]
        hu, hd = HB[step, i - 1], HB[step, i + 1]
        gu, gd = GB[step, i - 1], GB[step, i + 1]
        d_y = left(h) - h
        d_z = 1.0 + h - below(h)
        e_y = left(g) - g
        e_z = below(g) - g
        s_up, s_down = 0.5 * face(i - 1), 0.5 * face(i)
        c_y = right_half * d_y * e_y
        c_z = below_half * d_z * e_z
        grad_k = (
            s_down * ((hd - h) * (g - gd))
            + s_up * ((hu - h) * (g - gu))
            - (c_y + right(c_y))
            + (c_z + above(c_z))
            + forcing(step, i) * g
        )
        change = -lam * (dt * AB[step, i])
        n1 = n - 1.0
        m = 1.0 - 1.0 / n
        inv_n2 = 1.0 / (n * n)
        log_x, log_v, w, r = LG[step, i], LV[step, i], WW[step, i], RV[step, i]
        f = 1.0 - r
        wq = 2.0 * w * QQ[step, i]
        n1r = n1 * r
        fk = f * k
        grad_log = change * (n1r - n * f) - grad_k * ((0.5 * n1) * fk + n1r * wq)
        fl = f * log_x
        d_w = log_x - inv_n2 * log_v - m * fl
        grad_n = change * (1.0 / n1 + d_w - fl) - grad_k * (
            (0.5 * k) * (inv_n2 * log_v + m * fl) + wq * d_w
        )
        pair = (i - 1) // 2
        ACC[pair, 0] += fold(grad_k * k)
        ACC[pair, 1] += fold(grad_log + change)
        ACC[pair, 2] += fold(grad_n)
        if step == 0:
            return
        k_up = s_up * (KB[step, i - 1] + k)
        k_down = s_down * (k + KB[step, i + 1])
        f_y = right_half * (k + left(k)) * e_y
        f_z = below_half * (k + below(k)) * e_z
        lap = k_down * (gd - g) + k_up * (gu - g) + (f_y - right(f_y)) + (f_z - above(f_z))
        before = lam + lap + grad_log / h
        LAM[0, i] = before
        GB[0, i] = before * dt0 * IC[0, i]

    back1 = functools.partial(pull_back, 1, dt1)
    back0 = functools.partial(pull_back, 0, dt0)
    over(edges, back1)
    start(6)
    over(inner, back1)
    over(inner, back0)
    recv(6)
    over(edges, back0)

    zone_sums = None
    line = lax.broadcasted_iota(jnp.int32, (8, width), 0)
    for pair in range(2):
        sat, alpha, _ = params(1 + 2 * pair)
        grads = [
            jnp.sum(ACC[pair, 0], axis=0, keepdims=True) / sat,
            jnp.sum(ACC[pair, 1], axis=0, keepdims=True) / alpha,
            jnp.sum(ACC[pair, 2], axis=0, keepdims=True),
        ]
        block = jnp.zeros((8, width), F32)
        for place, grad in enumerate(grads):
            block = jnp.where(line == place, grad, block)
        part = nt_dot(block, OH[pair], HIGHEST)
        zone_sums = part if zone_sums is None else zone_sums + part
    loss = 0.5 * (jnp.sum(ACC[2, 0], keepdims=True) + scale * spread_sum)
    zone_line = lax.broadcasted_iota(jnp.int32, (8, zp), 0)
    SUMR[pos] = jnp.where(zone_line == 3, loss, zone_sums)

    def row_copy(k, src):
        return pltpu.make_async_remote_copy(
            src_ref=SUMR.at[src],
            dst_ref=SUMR.at[src],
            send_sem=sum_send.at[k],
            recv_sem=sum_recv.at[src],
            device_id=dev(lax.rem(pos + k, count)),
            device_id_type=pl.DeviceIdType.MESH,
        )

    def event_copy(k, src):
        return pltpu.make_async_remote_copy(
            src_ref=SUME.at[src],
            dst_ref=SUME.at[src],
            send_sem=ev_send.at[k],
            recv_sem=ev_recv.at[src],
            device_id=(lax.rem(me_event + k, groups), pos),
            device_id_type=pl.DeviceIdType.MESH,
        )

    for k in range(1, count):
        row_copy(k, pos).start()
    for k in range(1, count):
        row_copy(k, lax.rem(pos + k, count)).wait_recv()
    SUME[me_event] = jnp.sum(SUMR[...], axis=0)
    for k in range(1, groups):
        event_copy(k, me_event).start()
    for k in range(1, groups):
        event_copy(k, lax.rem(me_event + k, groups)).wait_recv()
    small_ref[...] = jnp.sum(SUME[...], axis=0)

    for number in range(LINKS):
        sent_pair(number, *pairs[number])
    for k in range(1, count):
        max_copy(0, k).wait_send()
        max_copy(1, k).wait_send()
        row_copy(k, pos).wait_send()
    for k in range(1, groups):
        event_copy(k, me_event).wait_send()


def local(
    initial_head,
    sat_conductivity,
    vg_alpha,
    vg_n,
    zone_map,
    forcing_plan,
    tensiometer_cells,
    tensiometer_heads,
):
    _, depth, rows, width = initial_head.shape
    zones = sat_conductivity.shape[0]
    zp = -(-zones // 128) * 128
    count = lax.axis_size("row")
    groups = lax.axis_size("event")
    sensors = tensiometer_cells.shape[1]
    vmem = pl.BlockSpec(memory_space=pltpu.VMEM)
    smem = pl.BlockSpec(memory_space=pltpu.SMEM)
    full = pltpu.VMEM((STEPS, rows + 2, depth, width), F32)
    single = pltpu.VMEM((rows + 2, depth, width), F32)
    dma = pltpu.SemaphoreType.DMA
    head, small = pl.pallas_call(
        functools.partial(kernel, count, groups, groups * initial_head.shape[0]),
        out_shape=(
            jax.ShapeDtypeStruct((rows, depth, width), F32),
            jax.ShapeDtypeStruct((8, zp), F32),
        ),
        in_specs=[vmem] * 5 + [smem] + [vmem] * 2,
        out_specs=(vmem, vmem),
        scratch_shapes=[
            full,
            full,
            full,
            full,
            full,
            full,
            full,
            full,
            full,
            full,
            full,
            single,
            single,
            pltpu.VMEM((4, 8, width), F32),
            pltpu.VMEM((8, zp), F32),
            pltpu.VMEM((2, zp, width), F32),
            pltpu.VMEM((2, 1, sensors), jnp.int32),
            pltpu.VMEM((2, 1, sensors), F32),
            pltpu.VMEM((STEPS, 8, width), F32),
            pltpu.VMEM((3, 3, 8, width), F32),
            pltpu.VMEM((STEPS, count, 8, 128), F32),
            pltpu.VMEM((count, 8, zp), F32),
            pltpu.VMEM((groups, 8, zp), F32),
            dma((LINKS, 2)),
            dma((LINKS, 2)),
            dma((STEPS, count)),
            dma((STEPS, count)),
            dma((count,)),
            dma((count,)),
            dma((groups,)),
            dma((groups,)),
        ],
        compiler_params=pltpu.CompilerParams(
            collective_id=0, has_side_effects=True, vmem_limit_bytes=48 * 1024 * 1024
        ),
    )(
        jnp.transpose(initial_head[0], (1, 0, 2)),
        sat_conductivity[None],
        vg_alpha[None],
        vg_n[None],
        zone_map,
        forcing_plan[0],
        tensiometer_cells,
        tensiometer_heads,
    )
    final = jnp.transpose(head, (1, 0, 2))[None]
    return (final, small[3, 0], small[0, :zones], small[1, :zones], small[2, :zones])


def solution(mesh):
    return jax.shard_map(
        local,
        mesh=mesh,
        in_specs=(
            P("event", None, "row", None),
            P(),
            P(),
            P(),
            P("row", None),
            P("event", None, "row"),
            P("event", "row"),
            P("event", "row"),
        ),
        out_specs=(P("event", None, "row", None), P(), P(), P(), P()),
        check_vma=False,
    )
```

profile of v0, /device:TPU:0, one launch (start us, length us, event | category | flops | bytes accessed | tf_op | source)
XLA Modules:
  0.0 40.1 jit_solution(10964871231987327488)
XLA Ops:
  0.6 1.0 %copy.16 = f32[1,48,4,384]{3,1,2,0:T(8,128)S(1)} copy(f32[1,48,4,384]{3,2,1,0:T(4,128)} %param.8) | data formatting | bytes 589824 | tf_op args[0]
  1.6 0.0 copy-start.2
  1.6 0.0 copy-start.3
  1.6 0.0 copy-start.5
  1.7 0.0 copy-start.6
  1.7 0.0 copy-start
  1.7 0.0 copy-start.1
  1.7 0.0 copy-start.4
  1.7 0.6 %copy-done.2 = s32[1,256]{1,0:T(1,128)S(1)} copy-done((s32[1,256]{1,0:T(1,128)S(1)}, s32[1,256]{1,0:T(1,128)}, u32[]{:S(2)}) %copy-start.2) | copy-done | bytes 1048
  2.3 0.0 copy-done.3
  2.3 0.0 copy-done.5
  2.3 0.0 copy-done.6
  2.3 0.0 copy-done
  2.4 0.0 copy-done.1
  2.4 0.0 copy-done.4
  2.4 35.9 %shard_map.119 = (f32[4,48,384]{2,1,0:T(8,128)S(1)}, f32[8,128]{1,0:T(8,128)S(1)}) custom-call(f32[4,48,384]{2,1,0:T(8,128)S(1)} %bitcast.19, f32[1,64]{1,0:T(1,128)S(1)} %bitcast.22, f32[1,64]{1,0:T(1,128)S(1)} %bitcast.23, f32[1,64]{1,0:T(1,128)S(1)} %bitcast.24, s32[2,192]{1,0:T(2,128)S(1)} %copy-done, s32[2,2]{1,0:T(2,128)S(1)} %bitcast.21, ...), custom_call_target="tpu_custom_call" | custom-call | tf_op jit(solution)/shard_map/pallas_call | solution.py:553
  38.3 0.5 %slice_bitcast_fusion = (f32[64]{0:T(128)}, f32[64]{0:T(128)}, f32[64]{0:T(128)}) fusion(f32[8,128]{1,0:T(8,128)S(1)} %get-tuple-element.8), kind=kLoop, calls=%fused_computation.1 | loop fusion | bytes 1536 | tf_op jit(solution)/shard_map/squeeze | solution.py:608
  38.8 0.5 %slice.12 = f32[1,1]{1,0:T(1,128)} slice(f32[8,128]{1,0:T(8,128)S(1)} %get-tuple-element.8), slice={[3:4], [0:1]} | slice | bytes 8 | tf_op jit(solution)/shard_map/slice | solution.py:608
  39.3 0.8 %copy.14 = f32[1,48,4,384]{3,2,1,0:T(4,128)} copy(f32[1,48,4,384]{3,1,2,0:T(8,128)S(1)} %bitcast.20) | data formatting | bytes 589824
Async XLA Ops:
  1.6 0.7 %copy-start.2 = (s32[1,256]{1,0:T(1,128)S(1)}, s32[1,256]{1,0:T(1,128)}, u32[]{:S(2)}) copy-start(s32[1,256]{1,0:T(1,128)} %cells_ref.1) | copy-start | bytes 3076
  1.6 0.7 %copy-start.3 = (f32[1,256]{1,0:T(1,128)S(1)}, f32[1,256]{1,0:T(1,128)}, u32[]{:S(2)}) copy-start(f32[1,256]{1,0:T(1,128)} %heads_ref.1) | copy-start | bytes 3076
  1.6 0.7 %copy-start.5 = (f32[64]{0:T(128)S(1)}, f32[64]{0:T(128)}, u32[]{:S(2)}) copy-start(f32[64]{0:T(128)} %param.10) | copy-start | bytes 772
  1.7 0.7 %copy-start.6 = (f32[64]{0:T(128)S(1)}, f32[64]{0:T(128)}, u32[]{:S(2)}) copy-start(f32[64]{0:T(128)} %param.11) | copy-start | bytes 772
  1.7 0.7 %copy-start = (s32[2,192]{1,0:T(2,128)S(1)}, s32[2,192]{1,0:T(2,128)}, u32[]{:S(2)}) copy-start(s32[2,192]{1,0:T(2,128)} %zone_ref.1) | copy-start | bytes 4612
  1.7 0.7 %copy-start.1 = (s32[1,2,2]{2,1,0:T(2,128)S(1)}, s32[1,2,2]{2,1,0:T(2,128)}, u32[]{:S(2)}) copy-start(s32[1,2,2]{2,1,0:T(2,128)} %param.13) | copy-start | bytes 52
  1.7 0.7 %copy-start.4 = (f32[64]{0:T(128)S(1)}, f32[64]{0:T(128)}, u32[]{:S(2)}) copy-start(f32[64]{0:T(128)} %param.9) | copy-start | bytes 772
where the time goes:
time: 40.3 us; the launch traced here: 40.1 us
  Pallas kernels  35.9 us (89%)
  local copies, waits for them, and re-layouts  3.55 us (9%)
  between operations  0.7 us (2%)
    pallas_call x1, Pallas kernels, local(): pl.pallas_call(functools.partial(kernel, count, groups, groups * initial_...  35.9 us
    unnamed x16, local copies, waits for them, and re-layouts  2.52 us

commit v1 on v0

--- a/solution.py
+++ b/solution.py
@@ -14,7 +14,8 @@
 HIGHEST = lax.Precision.HIGHEST
 F32 = jnp.float32
 BF16 = jnp.bfloat16
-LINKS = 7
+LINKS = 6
+DIRECT = 64
 
 
 def nt_dot(a, b, precision=None):
@@ -59,6 +60,8 @@
     OH,
     NC,
     NT,
+    SV,
+    NV,
     RATE,
     ACC,
     MX,
@@ -73,7 +76,7 @@
     ev_send,
     ev_recv,
 ):
-    rows, depth, width = x_ref.shape
+    depth, rows, width = x_ref.shape
     zp = OH.shape[1]
     zones = sat_ref.shape[1]
     pos = lax.axis_index("row")
@@ -86,19 +89,22 @@
     def dev(row):
         return (me_event, row)
 
+    total_devices = count * groups
+    direct = total_devices <= DIRECT
+    index = me_event * count + pos
+
+    def other(k):
+        at = lax.rem(index + k, total_devices)
+        return at // count, lax.rem(at, count)
+
     barrier = pltpu.get_barrier_semaphore()
-    for k in range(1, count):
-        pl.semaphore_signal(
-            barrier, 1, device_id=dev(lax.rem(pos + k, count)), device_id_type=pl.DeviceIdType.MESH
-        )
-    for k in range(1, groups):
-        pl.semaphore_signal(
-            barrier,
-            1,
-            device_id=(lax.rem(me_event + k, groups), pos),
-            device_id_type=pl.DeviceIdType.MESH,
-        )
-    pl.semaphore_wait(barrier, count - 1 + groups - 1)
+    if direct:
+        greeted = [other(k) for k in range(1, total_devices)]
+    else:
+        greeted = [dev(lax.rem(pos + k, count)) for k in range(1, count)]
+        greeted += [(lax.rem(me_event + k, groups), pos) for k in range(1, groups)]
+    for device in greeted:
+        pl.semaphore_signal(barrier, 1, device_id=device, device_id_type=pl.DeviceIdType.MESH)
 
     def link(number, side, src, dst):
         return pltpu.make_async_remote_copy(
@@ -138,13 +144,12 @@
             link(number, 1, *to_down).wait_send()
 
     pairs = [
-        ((x_ref.at[0], HB.at[0, rows + 1]), (x_ref.at[rows - 1], HB.at[0, 0])),
+        ((HB.at[0, 1], HB.at[0, rows + 1]), (HB.at[0, rows], HB.at[0, 0])),
         ((PB.at[1], PB.at[3]), (PB.at[2], PB.at[0])),
         ((cells_ref, NC.at[1]), (cells_ref, NC.at[0])),
         ((heads_ref, NT.at[1]), (heads_ref, NT.at[0])),
         ((AB.at[0, 1], AB.at[0, rows + 1]), (AB.at[0, rows], AB.at[0, 0])),
-        ((AB.at[1, 1], AB.at[1, rows + 1]), (AB.at[1, rows], AB.at[1, 0])),
-        ((GB.at[0, 1], GB.at[0, rows + 1]), (GB.at[0, rows], GB.at[0, 0])),
+        ((SV.at[0], NV.at[1]), (SV.at[1], NV.at[0])),
     ]
 
     def start(number):
@@ -153,9 +158,8 @@
     def recv(number):
         recv_pair(number, *pairs[number])
 
-    start(0)
-    start(2)
-    start(3)
+    for i in range(rows):
+        HB[0, i + 1] = x_ref[:, i, :]
 
     TAB[...] = jnp.zeros_like(TAB)
     TAB[0:1, :zones] = sat_ref[...]
@@ -167,31 +171,38 @@
         == lax.broadcasted_iota(jnp.int32, (blocks, width), 0)
     ).astype(F32)
     ids = jnp.dot(zone_ref[...].astype(F32), spread, preferred_element_type=F32, precision=HIGHEST)
-    zone_of = lax.broadcasted_iota(jnp.int32, (zp, width), 0).astype(F32)
+    packed = 2 * zones <= zp
+    period = zp // 2 if packed else zp
+    zone_of = (lax.broadcasted_iota(jnp.int32, (zp, width), 0) % period).astype(F32)
+    part_line = lax.broadcasted_iota(jnp.int32, (8, width), 0)
     for pair in range(2):
-        OH[pair] = jnp.where(zone_of == ids[pair : pair + 1], 1.0, 0.0)
-        PB[pair + 1] = jnp.dot(TAB[...], OH[pair], precision=HIGHEST, preferred_element_type=F32)
+        own_ids = ids[pair : pair + 1]
+        OH[pair + 1] = jnp.where(zone_of == own_ids, 1.0, 0.0)
+        block = jnp.dot(TAB[...], OH[pair + 1], precision=HIGHEST, preferred_element_type=F32)
+        PB[pair + 1] = jnp.where(part_line == 3, own_ids, block)
+    pl.semaphore_wait(barrier, len(greeted))
+    start(0)
     start(1)
+    start(2)
+    start(3)
 
     @pl.when(jnp.logical_not(has_up))
     def _():
-        HB[0, 0] = x_ref[0]
+        HB[0, 0] = HB[0, 1]
         PB[0] = PB[1]
         NC[0] = cells_ref[...]
         NT[0] = heads_ref[...]
-        for step in range(STEPS):
-            AB[step, 0] = jnp.zeros((depth, width), F32)
-        GB[0, 0] = jnp.zeros((depth, width), F32)
+        NV[0] = jnp.zeros_like(NV[0])
+        AB[0, 0] = jnp.zeros((depth, width), F32)
 
     @pl.when(jnp.logical_not(has_down))
     def _():
-        HB[0, rows + 1] = x_ref[rows - 1]
+        HB[0, rows + 1] = HB[0, rows]
         PB[3] = PB[2]
         NC[1] = cells_ref[...]
         NT[1] = heads_ref[...]
-        for step in range(STEPS):
-            AB[step, rows + 1] = jnp.zeros((depth, width), F32)
-        GB[0, rows + 1] = jnp.zeros((depth, width), F32)
+        NV[1] = jnp.zeros_like(NV[1])
+        AB[0, rows + 1] = jnp.zeros((depth, width), F32)
 
     ACC[...] = jnp.zeros_like(ACC)
 
@@ -318,17 +329,19 @@
     RATE[...] = jnp.zeros_like(RATE)
 
     def first_cell(i):
-        HB[0, i] = x_ref[i - 1]
-        cell(0, i, x_ref[i - 1])
+        cell(0, i, HB[0, i])
 
     over(own, first_cell)
     over(inner, functools.partial(flow, 0))
     recv(0)
     recv(1)
-    over(halo, lambda i: cell(0, i, HB[0, i]))
+    over(halo, first_cell)
     over(edges, functools.partial(flow, 0))
     send_rate(0)
     start(4)
+
+    for pair in (0, 3):
+        OH[pair] = jnp.where(zone_of == PB[pair][3:4], 1.0, 0.0)
 
     def places(cells):
         index = cells.astype(F32)
@@ -359,24 +372,33 @@
         line_of = lax.broadcasted_iota(jnp.int32, (lines, sensors), 0).astype(F32)
         hit = line_of == spot
         number = nt_dot(jnp.where(hit, 1.0, 0.0).astype(BF16), cols16)
+        total = put(targets, hit, cols16)
+        return number, total / jnp.maximum(number, 1.0), hit, cols
+
+    def put(values, hit, cols16):
         total = None
-        for piece in pieces(targets):
+        for piece in pieces(values):
             part = nt_dot(jnp.where(hit, piece.astype(F32), 0.0).astype(BF16), cols16)
             total = part if total is None else total + part
-        return number, total / jnp.maximum(number, 1.0), hit, cols
-
-    number, mean, hit, cols = counts(cells_ref[...], heads_ref[...], None)
+        return total
+
+    def take(field, hit, cols):
+        at_sensor = jnp.dot(field, cols, precision=HIGHEST, preferred_element_type=F32)
+        return jnp.sum(jnp.where(hit, at_sensor, 0.0), axis=0, keepdims=True)
+
+    number, mean, own_hit, own_cols = counts(cells_ref[...], heads_ref[...], None)
     WB[1 : rows + 1] = number.reshape(rows, depth, width)
     TM[1 : rows + 1] = mean.reshape(rows, depth, width)
-    at_sensor = jnp.dot(mean, cols, precision=HIGHEST, preferred_element_type=F32)
-    own_mean = jnp.sum(jnp.where(hit, at_sensor, 0.0), axis=0, keepdims=True)
+    own_mean = take(mean, own_hit, own_cols)
     spread_sum = jnp.sum((heads_ref[...] - own_mean) ** 2, keepdims=True)
     recv(2)
     recv(3)
+    halo_spots = []
     for side, wanted, place in ((0, rows - 1, 0), (1, 0, rows + 1)):
-        number, mean, _, _ = counts(NC[side], NT[side], wanted)
+        number, mean, hit, cols = counts(NC[side], NT[side], wanted)
         WB[place] = number
         TM[place] = mean
+        halo_spots.append((side, place, hit, cols))
 
     dt0 = step_size(0)
 
@@ -391,7 +413,12 @@
     over(halo, next_cell)
     over(edges, functools.partial(flow, 1))
     send_rate(1)
+    SV[0] = take(AB[1, 1], own_hit[:depth], own_cols)
+    SV[1] = take(AB[1, rows], own_hit[(rows - 1) * depth :], own_cols)
     start(5)
+    recv(5)
+    for side, place, hit, cols in halo_spots:
+        AB[1, place] = put(NV[side], hit, cols.astype(BF16)) / jnp.maximum(WB[place], 1.0)
     dt1 = step_size(1)
     scale = 1.0 / events
 
@@ -406,14 +433,37 @@
         head, square, pull = last_head(i)
         out_ref[i - 1] = head
         LAM[1, i] = pull
-        ACC[2, 0] += fold(square)
+        ACC[4, 0] += fold(square)
 
     over(own, finish)
-    recv(5)
     over(halo, lambda i: (last_head(i), None)[1])
 
+    def slopes(step, i, grad_k, change):
+        _, _, n = params(i)
+        n1 = n - 1.0
+        m = 1.0 - 1.0 / n
+        inv_n2 = 1.0 / (n * n)
+        k, log_x, log_v = KB[step, i], LG[step, i], LV[step, i]
+        w, r = WW[step, i], RV[step, i]
+        f = 1.0 - r
+        wq = 2.0 * w * QQ[step, i]
+        n1r = n1 * r
+        fl = f * log_x
+        d_w = log_x - inv_n2 * log_v - m * fl
+        by_log = -grad_k * ((0.5 * n1) * (f * k) + n1r * wq)
+        by_n = -grad_k * ((0.5 * k) * (inv_n2 * log_v + m * fl) + wq * d_w)
+        by_alpha = by_log
+        if change is not None:
+            by_log = by_log + change * (n1r - n * f)
+            by_n = by_n + change * (1.0 / n1 + d_w - fl)
+            by_alpha = by_log + change
+        pair = (i + 1) // 2
+        ACC[pair, 0] += fold(grad_k * k)
+        ACC[pair, 1] += fold(by_alpha)
+        ACC[pair, 2] += fold(by_n)
+        return by_log
+
     def pull_back(step, dt, i):
-        sat, alpha, n = params(i)
         h, k, g, lam = HB[step, i], KB[step, i], GB[step, i], LAM[step, i]
         hu, hd = HB[step, i - 1], HB[step, i + 1]
         gu, gd = GB[step, i - 1], GB[step, i + 1]
@@ -431,25 +481,7 @@
             + (c_z + above(c_z))
             + forcing(step, i) * g
         )
-        change = -lam * (dt * AB[step, i])
-        n1 = n - 1.0
-        m = 1.0 - 1.0 / n
-        inv_n2 = 1.0 / (n * n)
-        log_x, log_v, w, r = LG[step, i], LV[step, i], WW[step, i], RV[step, i]
-        f = 1.0 - r
-        wq = 2.0 * w * QQ[step, i]
-        n1r = n1 * r
-        fk = f * k
-        grad_log = change * (n1r - n * f) - grad_k * ((0.5 * n1) * fk + n1r * wq)
-        fl = f * log_x
-        d_w = log_x - inv_n2 * log_v - m * fl
-        grad_n = change * (1.0 / n1 + d_w - fl) - grad_k * (
-            (0.5 * k) * (inv_n2 * log_v + m * fl) + wq * d_w
-        )
-        pair = (i - 1) // 2
-        ACC[pair, 0] += fold(grad_k * k)
-        ACC[pair, 1] += fold(grad_log + change)
-        ACC[pair, 2] += fold(grad_n)
+        by_log = slopes(step, i, grad_k, -lam * (dt * AB[step, i]))
         if step == 0:
             return
         k_up = s_up * (KB[step, i - 1] + k)
@@ -457,23 +489,27 @@
         f_y = right_half * (k + left(k)) * e_y
         f_z = below_half * (k + below(k)) * e_z
         lap = k_down * (gd - g) + k_up * (gu - g) + (f_y - right(f_y)) + (f_z - above(f_z))
-        before = lam + lap + grad_log / h
+        before = lam + lap + by_log / h
         LAM[0, i] = before
         GB[0, i] = before * dt0 * IC[0, i]
 
-    back1 = functools.partial(pull_back, 1, dt1)
-    back0 = functools.partial(pull_back, 0, dt0)
-    over(edges, back1)
-    start(6)
-    over(inner, back1)
-    over(inner, back0)
-    recv(6)
-    over(edges, back0)
+    over(own, functools.partial(pull_back, 1, dt1))
+
+    GB[0, 0] = jnp.zeros((depth, width), F32)
+    GB[0, rows + 1] = jnp.zeros((depth, width), F32)
+    over(own, functools.partial(pull_back, 0, dt0))
+
+    def pull_halo(i):
+        near = jnp.where(i == 0, 1, rows)
+        half = jnp.where(i == 0, 0.5 * lower_open, 0.5 * upper_open)
+        slopes(0, i, half * ((HB[0, i] - HB[0, near]) * GB[0, near]), None)
+
+    over(halo, pull_halo)
 
     zone_sums = None
     line = lax.broadcasted_iota(jnp.int32, (8, width), 0)
-    for pair in range(2):
-        sat, alpha, _ = params(1 + 2 * pair)
+    for pair in range(4):
+        sat, alpha, _ = params(2 * pair - 1)
         grads = [
             jnp.sum(ACC[pair, 0], axis=0, keepdims=True) / sat,
             jnp.sum(ACC[pair, 1], axis=0, keepdims=True) / alpha,
@@ -484,9 +520,16 @@
             block = jnp.where(line == place, grad, block)
         part = nt_dot(block, OH[pair], HIGHEST)
         zone_sums = part if zone_sums is None else zone_sums + part
-    loss = 0.5 * (jnp.sum(ACC[2, 0], keepdims=True) + scale * spread_sum)
-    zone_line = lax.broadcasted_iota(jnp.int32, (8, zp), 0)
-    SUMR[pos] = jnp.where(zone_line == 3, loss, zone_sums)
+    loss = 0.5 * (jnp.sum(ACC[4, 0], keepdims=True) + scale * spread_sum)
+    if packed:
+        lane = lax.broadcasted_iota(jnp.int32, (1, zp), 1) < period
+        lines = [
+            jnp.where(lane, zone_sums[0:1], zone_sums[1:2]),
+            jnp.where(lane, zone_sums[2:3], loss),
+        ]
+    else:
+        lines = [zone_sums[0:1], zone_sums[1:2], zone_sums[2:3], loss + jnp.zeros((1, zp), F32)]
+    message = jnp.concatenate(lines, axis=0)
 
     def row_copy(k, src):
         return pltpu.make_async_remote_copy(
@@ -508,25 +551,49 @@
             device_id_type=pl.DeviceIdType.MESH,
         )
 
-    for k in range(1, count):
-        row_copy(k, pos).start()
-    for k in range(1, count):
-        row_copy(k, lax.rem(pos + k, count)).wait_recv()
-    SUME[me_event] = jnp.sum(SUMR[...], axis=0)
-    for k in range(1, groups):
-        event_copy(k, me_event).start()
-    for k in range(1, groups):
-        event_copy(k, lax.rem(me_event + k, groups)).wait_recv()
-    small_ref[...] = jnp.sum(SUME[...], axis=0)
+    def all_copy(k, src):
+        return pltpu.make_async_remote_copy(
+            src_ref=SUMR.at[src],
+            dst_ref=SUMR.at[src],
+            send_sem=sum_send.at[k],
+            recv_sem=sum_recv.at[src],
+            device_id=other(k),
+            device_id_type=pl.DeviceIdType.MESH,
+        )
+
+    if direct:
+        SUMR[index] = message
+        for k in range(1, total_devices):
+            all_copy(k, index).start()
+        for k in range(1, total_devices):
+            all_copy(k, lax.rem(index + k, total_devices)).wait_recv()
+        small_ref[...] = jnp.sum(SUMR[...], axis=0)
+    else:
+        SUMR[pos] = message
+        for k in range(1, count):
+            row_copy(k, pos).start()
+        for k in range(1, count):
+            row_copy(k, lax.rem(pos + k, count)).wait_recv()
+        SUME[me_event] = jnp.sum(SUMR[...], axis=0)
+        for k in range(1, groups):
+            event_copy(k, me_event).start()
+        for k in range(1, groups):
+            event_copy(k, lax.rem(me_event + k, groups)).wait_recv()
+        small_ref[...] = jnp.sum(SUME[...], axis=0)
 
     for number in range(LINKS):
         sent_pair(number, *pairs[number])
     for k in range(1, count):
         max_copy(0, k).wait_send()
         max_copy(1, k).wait_send()
-        row_copy(k, pos).wait_send()
-    for k in range(1, groups):
-        event_copy(k, me_event).wait_send()
+    if direct:
+        for k in range(1, total_devices):
+            all_copy(k, index).wait_send()
+    else:
+        for k in range(1, count):
+            row_copy(k, pos).wait_send()
+        for k in range(1, groups):
+            event_copy(k, me_event).wait_send()
 
 
 def local(
@@ -545,6 +612,8 @@
     count = lax.axis_size("row")
     groups = lax.axis_size("event")
     sensors = tensiometer_cells.shape[1]
+    lines = 2 if 2 * zones <= zp else 4
+    senders = count * groups if count * groups <= DIRECT else count
     vmem = pl.BlockSpec(memory_space=pltpu.VMEM)
     smem = pl.BlockSpec(memory_space=pltpu.SMEM)
     full = pltpu.VMEM((STEPS, rows + 2, depth, width), F32)
@@ -554,7 +623,7 @@
         functools.partial(kernel, count, groups, groups * initial_head.shape[0]),
         out_shape=(
             jax.ShapeDtypeStruct((rows, depth, width), F32),
-            jax.ShapeDtypeStruct((8, zp), F32),
+            jax.ShapeDtypeStruct((lines, zp), F32),
         ),
         in_specs=[vmem] * 5 + [smem] + [vmem] * 2,
         out_specs=(vmem, vmem),
@@ -574,20 +643,22 @@
             single,
             pltpu.VMEM((4, 8, width), F32),
             pltpu.VMEM((8, zp), F32),
-            pltpu.VMEM((2, zp, width), F32),
+            pltpu.VMEM((4, zp, width), F32),
             pltpu.VMEM((2, 1, sensors), jnp.int32),
             pltpu.VMEM((2, 1, sensors), F32),
+            pltpu.VMEM((2, 1, sensors), F32),
+            pltpu.VMEM((2, 1, sensors), F32),
             pltpu.VMEM((STEPS, 8, width), F32),
-            pltpu.VMEM((3, 3, 8, width), F32),
+            pltpu.VMEM((5, 3, 8, width), F32),
             pltpu.VMEM((STEPS, count, 8, 128), F32),
-            pltpu.VMEM((count, 8, zp), F32),
-            pltpu.VMEM((groups, 8, zp), F32),
+            pltpu.VMEM((senders, lines, zp), F32),
+            pltpu.VMEM((groups, lines, zp), F32),
             dma((LINKS, 2)),
             dma((LINKS, 2)),
             dma((STEPS, count)),
             dma((STEPS, count)),
-            dma((count,)),
-            dma((count,)),
+            dma((senders,)),
+            dma((senders,)),
             dma((groups,)),
             dma((groups,)),
         ],
@@ -595,7 +666,7 @@
             collective_id=0, has_side_effects=True, vmem_limit_bytes=48 * 1024 * 1024
         ),
     )(
-        jnp.transpose(initial_head[0], (1, 0, 2)),
+        initial_head[0],
         sat_conductivity[None],
         vg_alpha[None],
         vg_n[None],
@@ -605,6 +676,10 @@
         tensiometer_heads,
     )
     final = jnp.transpose(head, (1, 0, 2))[None]
+    if lines == 2:
+        half = zp // 2
+        grads = (small[0, :zones], small[0, half : half + zones], small[1, :zones])
+        return (final, small[1, half], *grads)
     return (final, small[3, 0], small[0, :zones], small[1, :zones], small[2, :zones])
 
 

time: 40.3 us -> 38.7 us (0.960)
  Pallas kernels: 35.9 us -> 34.2 us
    pallas_call x1, Pallas kernels: 35.9 us -> 34.2 us  [local(): pl.pallas_call(functools.partial(kernel, count, groups, groups * initial_...]
    unnamed x16 -> x17, local copies, waits for them, and re-layouts: 2.52 us -> 2.49 us
where the time goes in v1:
time: 38.7 us; the launch traced here: 38.5 us
  Pallas kernels  34.2 us (88%)
  local copies, waits for them, and re-layouts  3.66 us (9%)
  between operations  0.7 us (2%)
    pallas_call x1, Pallas kernels, local(): pl.pallas_call(functools.partial(kernel, count, groups, groups * initial_...  34.2 us
    unnamed x17, local copies, waits for them, and re-layouts  2.49 us

profile of v1, /device:TPU:0, one launch (start us, length us, event | category | flops | bytes accessed | tf_op | source)
XLA Modules:
  0.0 38.5 jit_solution(8361900290795559760)
XLA Ops:
  0.6 0.0 copy-start.6
  0.6 0.0 copy-start.7
  0.7 0.0 copy-start.3
  0.7 0.0 copy-start.4
  0.7 0.0 copy-start.1
  0.7 0.0 copy-start.2
  0.7 0.0 copy-start.5
  0.7 0.6 %copy-done.6 = f32[64]{0:T(128)S(1)} copy-done((f32[64]{0:T(128)S(1)}, f32[64]{0:T(128)}, u32[]{:S(2)}) %copy-start.6) | copy-done | bytes 280
  1.3 0.0 copy-done.7
  1.3 0.0 copy-done.3
  1.3 0.0 copy-done.4
  1.4 0.0 copy-done.1
  1.4 0.0 copy-done.2
  1.4 0.0 copy-done.5
  1.4 0.0 copy-start
  1.4 1.0 %copy-done = f32[1,48,4,384]{3,2,1,0:T(4,128)S(1)} copy-done((f32[1,48,4,384]{3,2,1,0:T(4,128)S(1)}, f32[1,48,4,384]{3,2,1,0:T(4,128)}, u32[]{:S(2)}) %copy-start) | copy-done | bytes 294936
  2.4 34.2 %shard_map.119 = (f32[4,48,384]{2,1,0:T(8,128)S(1)}, f32[2,128]{1,0:T(2,128)S(1)}) custom-call(f32[48,4,384]{2,1,0:T(4,128)S(1)} %bitcast.15, f32[1,64]{1,0:T(1,128)S(1)} %bitcast.18, f32[1,64]{1,0:T(1,128)S(1)} %bitcast.19, f32[1,64]{1,0:T(1,128)S(1)} %bitcast.20, s32[2,192]{1,0:T(2,128)S(1)} %copy-done.1, s32[2,2]{1,0:T(2,128)S(1)} %bitcast.17, ...), custom_call_target="tpu_custom_call" | custom-call | tf_op jit(solution)/shard_map/pallas_call | solution.py:622
  36.5 0.8 %copy.13 = f32[1,48,4,384]{3,2,1,0:T(4,128)} copy(f32[1,48,4,384]{3,1,2,0:T(8,128)S(1)} %bitcast.16) | data formatting | bytes 589824
  37.3 0.6 %slice.12 = f32[1,1]{1,0:T(1,128)} slice(f32[2,128]{1,0:T(2,128)S(1)} %get-tuple-element.8), slice={[1:2], [64:65]} | slice | bytes 8 | tf_op jit(solution)/shard_map/slice | solution.py:682
  37.9 0.6 %slice_bitcast_fusion = (f32[64]{0:T(128)}, f32[64]{0:T(128)}, f32[64]{0:T(128)}) fusion(f32[2,128]{1,0:T(2,128)S(1)} %get-tuple-element.8), kind=kLoop, calls=%fused_computation | loop fusion | bytes 1536 | tf_op jit(solution)/shard_map/squeeze | solution.py:681
Async XLA Ops:
  0.6 0.7 %copy-start.6 = (f32[64]{0:T(128)S(1)}, f32[64]{0:T(128)}, u32[]{:S(2)}) copy-start(f32[64]{0:T(128)} %param.10) | copy-start | bytes 772
  0.6 0.7 %copy-start.7 = (f32[64]{0:T(128)S(1)}, f32[64]{0:T(128)}, u32[]{:S(2)}) copy-start(f32[64]{0:T(128)} %param.11) | copy-start | bytes 772
  0.7 0.7 %copy-start.3 = (s32[1,256]{1,0:T(1,128)S(1)}, s32[1,256]{1,0:T(1,128)}, u32[]{:S(2)}) copy-start(s32[1,256]{1,0:T(1,128)} %cells_ref.1) | copy-start | bytes 3076
  0.7 0.7 %copy-start.4 = (f32[1,256]{1,0:T(1,128)S(1)}, f32[1,256]{1,0:T(1,128)}, u32[]{:S(2)}) copy-start(f32[1,256]{1,0:T(1,128)} %heads_ref.1) | copy-start | bytes 3076
  0.7 0.7 %copy-start.1 = (s32[2,192]{1,0:T(2,128)S(1)}, s32[2,192]{1,0:T(2,128)}, u32[]{:S(2)}) copy-start(s32[2,192]{1,0:T(2,128)} %zone_ref.1) | copy-start | bytes 4612
  0.7 0.7 %copy-start.2 = (s32[1,2,2]{2,1,0:T(2,128)S(1)}, s32[1,2,2]{2,1,0:T(2,128)}, u32[]{:S(2)}) copy-start(s32[1,2,2]{2,1,0:T(2,128)} %param.13) | copy-start | bytes 52
  0.7 0.7 %copy-start.5 = (f32[64]{0:T(128)S(1)}, f32[64]{0:T(128)}, u32[]{:S(2)}) copy-start(f32[64]{0:T(128)} %param.9) | copy-start | bytes 772
  1.4 1.0 %copy-start = (f32[1,48,4,384]{3,2,1,0:T(4,128)S(1)}, f32[1,48,4,384]{3,2,1,0:T(4,128)}, u32[]{:S(2)}) copy-start(f32[1,48,4,384]{3,2,1,0:T(4,128)} %param.8) | copy-start | bytes 884740

commit v2 on v1

--- a/solution.py
+++ b/solution.py
@@ -14,14 +14,26 @@
 HIGHEST = lax.Precision.HIGHEST
 F32 = jnp.float32
 BF16 = jnp.bfloat16
+LAYERS = 16
+PAD = 8
 LINKS = 6
 DIRECT = 64
 
 
-def nt_dot(a, b, precision=None):
-    return lax.dot_general(
-        a, b, (((1,), (1,)), ((), ())), precision=precision, preferred_element_type=F32
-    )
+def nt_dot(a, b):
+    return lax.dot_general(a, b, (((1,), (1,)), ((), ())), preferred_element_type=F32)
+
+
+def pieces(t):
+    one = t.astype(BF16).astype(F32)
+    two = (t - one).astype(BF16).astype(F32)
+    return one, two, t - one - two
+
+
+def three(t, product):
+    size = t.shape[0]
+    out = product(jnp.concatenate(pieces(t), axis=0).astype(BF16))
+    return out[:size] + out[size : 2 * size] + out[2 * size :]
 
 
 def fold(x):
@@ -62,6 +74,7 @@
     NT,
     SV,
     NV,
+    XV,
     RATE,
     ACC,
     MX,
@@ -75,7 +88,10 @@
     sum_recv,
     ev_send,
     ev_recv,
+    x_sem,
 ):
+    fetch = pltpu.make_async_copy(x_ref, XV, x_sem)
+    fetch.start()
     depth, rows, width = x_ref.shape
     zp = OH.shape[1]
     zones = sat_ref.shape[1]
@@ -106,6 +122,8 @@
     for device in greeted:
         pl.semaphore_signal(barrier, 1, device_id=device, device_id_type=pl.DeviceIdType.MESH)
 
+    deep = pl.ds(PAD, depth)
+
     def link(number, side, src, dst):
         return pltpu.make_async_remote_copy(
             src_ref=src,
@@ -144,7 +162,7 @@
             link(number, 1, *to_down).wait_send()
 
     pairs = [
-        ((HB.at[0, 1], HB.at[0, rows + 1]), (HB.at[0, rows], HB.at[0, 0])),
+        ((HB.at[0, 1, deep], HB.at[0, rows + 1, deep]), (HB.at[0, rows, deep], HB.at[0, 0, deep])),
         ((PB.at[1], PB.at[3]), (PB.at[2], PB.at[0])),
         ((cells_ref, NC.at[1]), (cells_ref, NC.at[0])),
         ((heads_ref, NT.at[1]), (heads_ref, NT.at[0])),
@@ -157,9 +175,6 @@
 
     def recv(number):
         recv_pair(number, *pairs[number])
-
-    for i in range(rows):
-        HB[0, i + 1] = x_ref[:, i, :]
 
     TAB[...] = jnp.zeros_like(TAB)
     TAB[0:1, :zones] = sat_ref[...]
@@ -170,16 +185,27 @@
         lax.broadcasted_iota(jnp.int32, (blocks, width), 1) // 2
         == lax.broadcasted_iota(jnp.int32, (blocks, width), 0)
     ).astype(F32)
-    ids = jnp.dot(zone_ref[...].astype(F32), spread, preferred_element_type=F32, precision=HIGHEST)
+    exact = None if zones <= 256 else HIGHEST
+    ids = jnp.dot(
+        zone_ref[...].astype(F32), spread, preferred_element_type=F32, precision=exact
+    )
     packed = 2 * zones <= zp
     period = zp // 2 if packed else zp
     zone_of = (lax.broadcasted_iota(jnp.int32, (zp, width), 0) % period).astype(F32)
     part_line = lax.broadcasted_iota(jnp.int32, (8, width), 0)
     for pair in range(2):
         own_ids = ids[pair : pair + 1]
-        OH[pair + 1] = jnp.where(zone_of == own_ids, 1.0, 0.0)
-        block = jnp.dot(TAB[...], OH[pair + 1], precision=HIGHEST, preferred_element_type=F32)
+        OH[pair + 1] = jnp.where(zone_of == own_ids, 1.0, 0.0).astype(BF16)
+        block = three(TAB[...], lambda t: jnp.dot(t, OH[pair + 1], preferred_element_type=F32))
         PB[pair + 1] = jnp.where(part_line == 3, own_ids, block)
+    for ref in (HB, KB, GB):
+        for step in range(STEPS):
+            for i in range(1, rows + 1):
+                ref[step, i, 0:PAD] = jnp.zeros((PAD, width), F32)
+                ref[step, i, PAD + depth :] = jnp.zeros((PAD, width), F32)
+    fetch.wait()
+    for i in range(rows):
+        HB[0, i + 1, deep] = XV[:, i, :]
     pl.semaphore_wait(barrier, len(greeted))
     start(0)
     start(1)
@@ -188,7 +214,7 @@
 
     @pl.when(jnp.logical_not(has_up))
     def _():
-        HB[0, 0] = HB[0, 1]
+        HB[0, 0, deep] = HB[0, 1, deep]
         PB[0] = PB[1]
         NC[0] = cells_ref[...]
         NT[0] = heads_ref[...]
@@ -197,7 +223,7 @@
 
     @pl.when(jnp.logical_not(has_down))
     def _():
-        HB[0, rows + 1] = HB[0, rows]
+        HB[0, rows + 1, deep] = HB[0, rows, deep]
         PB[3] = PB[2]
         NC[1] = cells_ref[...]
         NT[1] = heads_ref[...]
@@ -209,20 +235,43 @@
     column = lax.broadcasted_iota(jnp.int32, (1, width), 1)
     layer = lax.broadcasted_iota(jnp.int32, (depth, 1), 0)
     right_half = jnp.where(column < width - 1, 0.5, 0.0)
-    below_half = jnp.where(layer < depth - 1, 0.5, 0.0)
-    ends = jnp.where((layer == 0) | (layer == depth - 1), 1.0, 0.0)
+    chunk_layer = lax.broadcasted_iota(jnp.int32, (LAYERS, 1), 0)
+
+    class Chunk:
+        def __init__(self, first):
+            last = first + LAYERS == depth
+            self.bare = pl.ds(first, LAYERS)
+            self.here = pl.ds(PAD + first, LAYERS)
+            self.above = pl.ds(PAD + first - 1, LAYERS)
+            self.below = pl.ds(PAD + first + 1, LAYERS)
+            self.top = chunk_layer == 0 if first == 0 else None
+            self.bottom = chunk_layer == LAYERS - 1 if last else None
+            self.half_above = 0.5 if self.top is None else jnp.where(self.top, 0.0, 0.5)
+            self.half_below = 0.5 if self.bottom is None else jnp.where(self.bottom, 0.0, 0.5)
+
+        def forcing(self, level, v):
+            out = 0.0
+            if self.top is not None:
+                out = out + jnp.where(self.top, level * IRRIGATION, 0.0) * v
+            if self.bottom is not None:
+                out = out - jnp.where(self.bottom, v, 0.0)
+            return out
+
+        def ends(self, v):
+            out = 0.0
+            if self.top is not None:
+                out = out + jnp.where(self.top, v, 0.0)
+            if self.bottom is not None:
+                out = out + jnp.where(self.bottom, v, 0.0)
+            return out
+
+    chunks = [Chunk(first) for first in range(0, depth, LAYERS)]
 
     def left(v):
         return pltpu.roll(v, width - 1, 1)
 
     def right(v):
         return pltpu.roll(v, 1, 1)
-
-    def above(v):
-        return pltpu.roll(v, 1, 0)
-
-    def below(v):
-        return pltpu.roll(v, depth - 1, 0)
 
     def over(indices, body):
         first, stride, number = indices
@@ -245,50 +294,64 @@
     def face(i):
         return jnp.where(i == 0, lower_open, jnp.where(i == rows, upper_open, 1.0))
 
-    def forcing(step, i):
-        level = jnp.where(i > 2, plan_ref[step, 1], plan_ref[step, 0]).astype(F32)
-        return jnp.where(layer == 0, level * IRRIGATION, jnp.where(layer == depth - 1, -1.0, 0.0))
-
-    def cell(step, i, head):
+    def level_of(step, i):
+        return jnp.where(i > 2, plan_ref[step, 1], plan_ref[step, 0]).astype(F32)
+
+    def cell(step, i):
         sat, alpha, n = params(i)
         m = 1.0 - 1.0 / n
-        x = alpha * -head
-        log_x = jnp.log(x)
-        power = jnp.exp((n - 1.0) * log_x)
-        v = 1.0 + x * power
-        log_v = jnp.log(v)
-        root = jnp.exp((-0.5 * m) * log_v)
-        w = power * (root * root)
-        rest = 1.0 - w
-        q = sat * root * rest
-        KB[step, i] = q * rest
-        IC[step, i] = v / ((WATER_RANGE * (n - 1.0) * alpha) * w)
-        LG[step, i] = log_x
-        LV[step, i] = log_v
-        WW[step, i] = w
-        RV[step, i] = 1.0 / v
-        QQ[step, i] = q
+        n1 = n - 1.0
+        half_m = -0.5 * m
+        scale = WATER_RANGE * n1 * alpha
+        for c in chunks:
+            if step == 0:
+                head = HB[0, i, c.here]
+            else:
+                head = HB[0, i, c.here] + dt0 * AB[0, i, c.bare]
+                HB[1, i, c.here] = head
+            x = alpha * -head
+            log_x = jnp.log(x)
+            power = jnp.exp(n1 * log_x)
+            v = 1.0 + x * power
+            log_v = jnp.log(v)
+            root = jnp.exp(half_m * log_v)
+            w = power * (root * root)
+            rest = 1.0 - w
+            q = sat * root * rest
+            KB[step, i, c.here] = q * rest
+            IC[step, i, c.bare] = v / (scale * w)
+            LG[step, i, c.bare] = log_x
+            LV[step, i, c.bare] = log_v
+            WW[step, i, c.bare] = w
+            RV[step, i, c.bare] = 1.0 / v
+            QQ[step, i, c.bare] = q
 
     def flow(step, i):
-        h, k = HB[step, i], KB[step, i]
-        inv = IC[step, i]
-        k_up = (0.5 * face(i - 1)) * (KB[step, i - 1] + k)
-        k_down = (0.5 * face(i)) * (k + KB[step, i + 1])
-        k_y = right_half * (k + left(k))
-        k_z = below_half * (k + below(k))
-        f_y = k_y * (left(h) - h)
-        f_z = k_z * (1.0 + h - below(h))
-        net = (
-            k_down * (HB[step, i + 1] - h)
-            + k_up * (HB[step, i - 1] - h)
-            + (f_y - right(f_y))
-            + (above(f_z) - f_z)
-            + forcing(step, i) * k
-        )
-        total = k_up + k_down + (k_y + right(k_y)) + (k_z + above(k_z)) + ends * k
-        AB[step, i] = net * inv
-        rate = jnp.max((total * inv).reshape(depth // 8, 8, width), axis=0)
-        RATE[step] = jnp.maximum(RATE[step], rate)
+        s_up, s_down = 0.5 * face(i - 1), 0.5 * face(i)
+        level = level_of(step, i)
+        top_rate = None
+        for c in chunks:
+            h, k = HB[step, i, c.here], KB[step, i, c.here]
+            inv = IC[step, i, c.bare]
+            k_up = s_up * (KB[step, i - 1, c.here] + k)
+            k_down = s_down * (k + KB[step, i + 1, c.here])
+            k_y = right_half * (k + left(k))
+            f_y = k_y * (left(h) - h)
+            k_above = c.half_above * (KB[step, i, c.above] + k)
+            k_below = c.half_below * (k + KB[step, i, c.below])
+            net = (
+                k_down * (HB[step, i + 1, c.here] - h)
+                + k_up * (HB[step, i - 1, c.here] - h)
+                + (f_y - right(f_y))
+                + k_above * (1.0 + HB[step, i, c.above] - h)
+                - k_below * (1.0 + h - HB[step, i, c.below])
+                + c.forcing(level, k)
+            )
+            total = k_up + k_down + (k_y + right(k_y)) + (k_above + k_below) + c.ends(k)
+            AB[step, i, c.bare] = net * inv
+            rate = jnp.max((total * inv).reshape(LAYERS // 8, 8, width), axis=0)
+            top_rate = rate if top_rate is None else jnp.maximum(top_rate, rate)
+        RATE[step] = jnp.maximum(RATE[step], top_rate)
 
     def max_copy(step, k):
         return pltpu.make_async_remote_copy(
@@ -329,7 +392,7 @@
     RATE[...] = jnp.zeros_like(RATE)
 
     def first_cell(i):
-        cell(0, i, HB[0, i])
+        cell(0, i)
 
     over(own, first_cell)
     over(inner, functools.partial(flow, 0))
@@ -341,7 +404,7 @@
     start(4)
 
     for pair in (0, 3):
-        OH[pair] = jnp.where(zone_of == PB[pair][3:4], 1.0, 0.0)
+        OH[pair] = jnp.where(zone_of == PB[pair][3:4], 1.0, 0.0).astype(BF16)
 
     def places(cells):
         index = cells.astype(F32)
@@ -350,19 +413,12 @@
         level = jnp.floor((line + 0.5) * (1.0 / rows))
         return level, line - rows * level, col
 
-    def pieces(t):
-        one = t.astype(BF16)
-        rest = t - one.astype(F32)
-        two = rest.astype(BF16)
-        return one, two, (rest - two.astype(F32)).astype(BF16)
-
     sensors = cells_ref.shape[1]
     col_of = lax.broadcasted_iota(jnp.int32, (width, sensors), 0).astype(F32)
 
     def counts(cells, targets, wanted):
         level, row, col = places(cells)
-        cols = jnp.where(col_of == col, 1.0, 0.0)
-        cols16 = cols.astype(BF16)
+        cols16 = jnp.where(col_of == col, 1.0, 0.0).astype(BF16)
         if wanted is None:
             spot = row * depth + level
             lines = rows * depth
@@ -371,26 +427,30 @@
             lines = depth
         line_of = lax.broadcasted_iota(jnp.int32, (lines, sensors), 0).astype(F32)
         hit = line_of == spot
-        number = nt_dot(jnp.where(hit, 1.0, 0.0).astype(BF16), cols16)
-        total = put(targets, hit, cols16)
-        return number, total / jnp.maximum(number, 1.0), hit, cols
+        parts = [jnp.ones_like(targets), *pieces(targets)]
+        out = nt_dot(stack(hit, parts), cols16)
+        number = out[:lines]
+        total = out[lines : 2 * lines] + out[2 * lines : 3 * lines] + out[3 * lines :]
+        return number, total / jnp.maximum(number, 1.0), hit, cols16
+
+    def stack(hit, parts):
+        return jnp.concatenate([jnp.where(hit, part, 0.0) for part in parts], axis=0).astype(BF16)
 
     def put(values, hit, cols16):
-        total = None
-        for piece in pieces(values):
-            part = nt_dot(jnp.where(hit, piece.astype(F32), 0.0).astype(BF16), cols16)
-            total = part if total is None else total + part
-        return total
-
-    def take(field, hit, cols):
-        at_sensor = jnp.dot(field, cols, precision=HIGHEST, preferred_element_type=F32)
-        return jnp.sum(jnp.where(hit, at_sensor, 0.0), axis=0, keepdims=True)
+        lines = hit.shape[0]
+        out = nt_dot(stack(hit, pieces(values)), cols16)
+        return out[:lines] + out[lines : 2 * lines] + out[2 * lines :]
+
+    def take(field, hit, cols16):
+        at_sensor = three(field, lambda t: jnp.dot(t, cols16, preferred_element_type=F32))
+        return jnp.where(hit, at_sensor, 0.0)
+
+    def column_sum(v):
+        return jnp.sum(v, axis=0, keepdims=True)
 
     number, mean, own_hit, own_cols = counts(cells_ref[...], heads_ref[...], None)
     WB[1 : rows + 1] = number.reshape(rows, depth, width)
     TM[1 : rows + 1] = mean.reshape(rows, depth, width)
-    own_mean = take(mean, own_hit, own_cols)
-    spread_sum = jnp.sum((heads_ref[...] - own_mean) ** 2, keepdims=True)
     recv(2)
     recv(3)
     halo_spots = []
@@ -403,9 +463,7 @@
     dt0 = step_size(0)
 
     def next_cell(i):
-        head = HB[0, i] + dt0 * AB[0, i]
-        HB[1, i] = head
-        cell(1, i, head)
+        cell(1, i)
 
     over(own, next_cell)
     over(inner, functools.partial(flow, 1))
@@ -413,20 +471,25 @@
     over(halo, next_cell)
     over(edges, functools.partial(flow, 1))
     send_rate(1)
-    SV[0] = take(AB[1, 1], own_hit[:depth], own_cols)
-    SV[1] = take(AB[1, rows], own_hit[(rows - 1) * depth :], own_cols)
+    brims = jnp.concatenate([AB[1, 1], AB[1, rows]], axis=0)
+    brim_hit = jnp.concatenate([own_hit[:depth], own_hit[(rows - 1) * depth :]], axis=0)
+    picked = take(brims, brim_hit, own_cols)
+    SV[0] = column_sum(picked[:depth])
+    SV[1] = column_sum(picked[depth:])
     start(5)
+    own_mean = column_sum(take(TM[1 : rows + 1].reshape(rows * depth, width), own_hit, own_cols))
+    spread_sum = jnp.sum((heads_ref[...] - own_mean) ** 2, keepdims=True)
     recv(5)
     for side, place, hit, cols in halo_spots:
-        AB[1, place] = put(NV[side], hit, cols.astype(BF16)) / jnp.maximum(WB[place], 1.0)
+        AB[1, place] = put(NV[side], hit, cols) / jnp.maximum(WB[place], 1.0)
     dt1 = step_size(1)
     scale = 1.0 / events
 
     def last_head(i):
-        head = HB[1, i] + dt1 * AB[1, i]
+        head = HB[1, i, deep] + dt1 * AB[1, i]
         off = head - TM[i]
         pull = (scale * WB[i]) * off
-        GB[1, i] = pull * dt1 * IC[1, i]
+        GB[1, i, deep] = pull * dt1 * IC[1, i]
         return head, off * pull, pull
 
     def finish(i):
@@ -438,71 +501,90 @@
     over(own, finish)
     over(halo, lambda i: (last_head(i), None)[1])
 
-    def slopes(step, i, grad_k, change):
+    def slopes(step, i, grad_k_of, change_of):
         _, _, n = params(i)
         n1 = n - 1.0
         m = 1.0 - 1.0 / n
         inv_n2 = 1.0 / (n * n)
-        k, log_x, log_v = KB[step, i], LG[step, i], LV[step, i]
-        w, r = WW[step, i], RV[step, i]
-        f = 1.0 - r
-        wq = 2.0 * w * QQ[step, i]
-        n1r = n1 * r
-        fl = f * log_x
-        d_w = log_x - inv_n2 * log_v - m * fl
-        by_log = -grad_k * ((0.5 * n1) * (f * k) + n1r * wq)
-        by_n = -grad_k * ((0.5 * k) * (inv_n2 * log_v + m * fl) + wq * d_w)
-        by_alpha = by_log
-        if change is not None:
-            by_log = by_log + change * (n1r - n * f)
-            by_n = by_n + change * (1.0 / n1 + d_w - fl)
-            by_alpha = by_log + change
+        inv_n1 = 1.0 / n1
+        half_n1 = 0.5 * n1
+        sums = None
+        for c in chunks:
+            k, log_x, log_v = KB[step, i, c.here], LG[step, i, c.bare], LV[step, i, c.bare]
+            w, r = WW[step, i, c.bare], RV[step, i, c.bare]
+            grad_k = grad_k_of(c)
+            f = 1.0 - r
+            wq = 2.0 * w * QQ[step, i, c.bare]
+            n1r = n1 * r
+            fl = f * log_x
+            log_v = inv_n2 * log_v
+            mfl = m * fl
+            d_w = log_x - log_v - mfl
+            by_log = -grad_k * (half_n1 * (f * k) + n1r * wq)
+            by_n = -grad_k * ((0.5 * k) * (log_v + mfl) + wq * d_w)
+            by_alpha = by_log
+            if change_of is not None:
+                change = change_of(c)
+                by_log = by_log + change * (n1r - n * f)
+                by_n = by_n + change * (inv_n1 + d_w - fl)
+                by_alpha = by_log + change
+            parts = [fold(grad_k * k), fold(by_alpha), fold(by_n)]
+            sums = parts if sums is None else [a + b for a, b in zip(sums, parts)]
+            yield c, by_log
         pair = (i + 1) // 2
-        ACC[pair, 0] += fold(grad_k * k)
-        ACC[pair, 1] += fold(by_alpha)
-        ACC[pair, 2] += fold(by_n)
-        return by_log
+        for place in range(3):
+            ACC[pair, place] += sums[place]
 
     def pull_back(step, dt, i):
-        h, k, g, lam = HB[step, i], KB[step, i], GB[step, i], LAM[step, i]
-        hu, hd = HB[step, i - 1], HB[step, i + 1]
-        gu, gd = GB[step, i - 1], GB[step, i + 1]
-        d_y = left(h) - h
-        d_z = 1.0 + h - below(h)
-        e_y = left(g) - g
-        e_z = below(g) - g
         s_up, s_down = 0.5 * face(i - 1), 0.5 * face(i)
-        c_y = right_half * d_y * e_y
-        c_z = below_half * d_z * e_z
-        grad_k = (
-            s_down * ((hd - h) * (g - gd))
-            + s_up * ((hu - h) * (g - gu))
-            - (c_y + right(c_y))
-            + (c_z + above(c_z))
-            + forcing(step, i) * g
-        )
-        by_log = slopes(step, i, grad_k, -lam * (dt * AB[step, i]))
-        if step == 0:
-            return
-        k_up = s_up * (KB[step, i - 1] + k)
-        k_down = s_down * (k + KB[step, i + 1])
-        f_y = right_half * (k + left(k)) * e_y
-        f_z = below_half * (k + below(k)) * e_z
-        lap = k_down * (gd - g) + k_up * (gu - g) + (f_y - right(f_y)) + (f_z - above(f_z))
-        before = lam + lap + by_log / h
-        LAM[0, i] = before
-        GB[0, i] = before * dt0 * IC[0, i]
+        level = level_of(step, i)
+
+        def grad_k_of(c):
+            h, g = HB[step, i, c.here], GB[step, i, c.here]
+            c_y = right_half * (left(h) - h) * (left(g) - g)
+            return (
+                s_down * ((HB[step, i + 1, c.here] - h) * (g - GB[step, i + 1, c.here]))
+                + s_up * ((HB[step, i - 1, c.here] - h) * (g - GB[step, i - 1, c.here]))
+                - (c_y + right(c_y))
+                + c.half_above * (1.0 + HB[step, i, c.above] - h) * (g - GB[step, i, c.above])
+                + c.half_below * (1.0 + h - HB[step, i, c.below]) * (GB[step, i, c.below] - g)
+                + c.forcing(level, g)
+            )
+
+        def change_of(c):
+            return -LAM[step, i, c.bare] * (dt * AB[step, i, c.bare])
+
+        for c, by_log in slopes(step, i, grad_k_of, change_of):
+            if step == 0:
+                continue
+            h, k, g = HB[step, i, c.here], KB[step, i, c.here], GB[step, i, c.here]
+            f_y = right_half * (k + left(k)) * (left(g) - g)
+            lap = (
+                s_down * (k + KB[step, i + 1, c.here]) * (GB[step, i + 1, c.here] - g)
+                + s_up * (KB[step, i - 1, c.here] + k) * (GB[step, i - 1, c.here] - g)
+                + (f_y - right(f_y))
+                + c.half_above * (KB[step, i, c.above] + k) * (GB[step, i, c.above] - g)
+                + c.half_below * (k + KB[step, i, c.below]) * (GB[step, i, c.below] - g)
+            )
+            before = LAM[step, i, c.bare] + lap + by_log / h
+            LAM[0, i, c.bare] = before
+            GB[0, i, c.here] = before * dt0 * IC[0, i, c.bare]
 
     over(own, functools.partial(pull_back, 1, dt1))
 
-    GB[0, 0] = jnp.zeros((depth, width), F32)
-    GB[0, rows + 1] = jnp.zeros((depth, width), F32)
+    GB[0, 0] = jnp.zeros_like(GB[0, 0])
+    GB[0, rows + 1] = jnp.zeros_like(GB[0, 0])
     over(own, functools.partial(pull_back, 0, dt0))
 
     def pull_halo(i):
         near = jnp.where(i == 0, 1, rows)
         half = jnp.where(i == 0, 0.5 * lower_open, 0.5 * upper_open)
-        slopes(0, i, half * ((HB[0, i] - HB[0, near]) * GB[0, near]), None)
+
+        def grad_k_of(c):
+            return half * ((HB[0, i, c.here] - HB[0, near, c.here]) * GB[0, near, c.here])
+
+        for _ in slopes(0, i, grad_k_of, None):
+            pass
 
     over(halo, pull_halo)
 
@@ -518,7 +600,7 @@
         block = jnp.zeros((8, width), F32)
         for place, grad in enumerate(grads):
             block = jnp.where(line == place, grad, block)
-        part = nt_dot(block, OH[pair], HIGHEST)
+        part = three(block, lambda t: nt_dot(t, OH[pair]))
         zone_sums = part if zone_sums is None else zone_sums + part
     loss = 0.5 * (jnp.sum(ACC[4, 0], keepdims=True) + scale * spread_sum)
     if packed:
@@ -616,6 +698,7 @@
     senders = count * groups if count * groups <= DIRECT else count
     vmem = pl.BlockSpec(memory_space=pltpu.VMEM)
     smem = pl.BlockSpec(memory_space=pltpu.SMEM)
+    deep = pltpu.VMEM((STEPS, rows + 2, depth + 2 * PAD, width), F32)
     full = pltpu.VMEM((STEPS, rows + 2, depth, width), F32)
     single = pltpu.VMEM((rows + 2, depth, width), F32)
     dma = pltpu.SemaphoreType.DMA
@@ -625,9 +708,11 @@
             jax.ShapeDtypeStruct((rows, depth, width), F32),
             jax.ShapeDtypeStruct((lines, zp), F32),
         ),
-        in_specs=[vmem] * 5 + [smem] + [vmem] * 2,
+        in_specs=[pl.BlockSpec(memory_space=pl.ANY)] + [vmem] * 4 + [smem] + [vmem] * 2,
         out_specs=(vmem, vmem),
         scratch_shapes=[
+            deep,
+            deep,
             full,
             full,
             full,
@@ -635,19 +720,18 @@
             full,
             full,
             full,
-            full,
-            full,
-            full,
+            deep,
             full,
             single,
             single,
             pltpu.VMEM((4, 8, width), F32),
             pltpu.VMEM((8, zp), F32),
-            pltpu.VMEM((4, zp, width), F32),
+            pltpu.VMEM((4, zp, width), BF16),
             pltpu.VMEM((2, 1, sensors), jnp.int32),
             pltpu.VMEM((2, 1, sensors), F32),
             pltpu.VMEM((2, 1, sensors), F32),
             pltpu.VMEM((2, 1, sensors), F32),
+            pltpu.VMEM((depth, rows, width), F32),
             pltpu.VMEM((STEPS, 8, width), F32),
             pltpu.VMEM((5, 3, 8, width), F32),
             pltpu.VMEM((STEPS, count, 8, 128), F32),
@@ -661,6 +745,7 @@
             dma((senders,)),
             dma((groups,)),
             dma((groups,)),
+            dma,
         ],
         compiler_params=pltpu.CompilerParams(
             collective_id=0, has_side_effects=True, vmem_limit_bytes=48 * 1024 * 1024

time: 38.7 us -> 37.2 us (0.961)
  Pallas kernels: 34.2 us -> 32.7 us
    pallas_call x1, Pallas kernels: 34.2 us -> 32.7 us  [local(): pl.pallas_call(functools.partial(kernel, count, groups, groups * initial_...]
where the time goes in v2:
time: 37.2 us; the launch traced here: 37 us
  Pallas kernels  32.7 us (88%)
  local copies, waits for them, and re-layouts  3.66 us (10%)
  between operations  0.7 us (2%)
    pallas_call x1, Pallas kernels, local(): pl.pallas_call(functools.partial(kernel, count, groups, groups * initial_...  32.7 us
    unnamed x17, local copies, waits for them, and re-layouts  2.49 us

profile of v2, /device:TPU:0, one launch (start us, length us, event | category | flops | bytes accessed | tf_op | source)
XLA Modules:
  0.0 37.0 jit_solution(4006810252117019916)
XLA Ops:
  0.6 0.0 copy-start.6
  0.6 0.0 copy-start.7
  0.7 0.0 copy-start.3
  0.7 0.0 copy-start.4
  0.7 0.0 copy-start.1
  0.7 0.0 copy-start.2
  0.7 0.0 copy-start.5
  0.7 0.6 %copy-done.6 = f32[64]{0:T(128)S(1)} copy-done((f32[64]{0:T(128)S(1)}, f32[64]{0:T(128)}, u32[]{:S(2)}) %copy-start.6) | copy-done | bytes 280
  1.3 0.0 copy-done.7
  1.3 0.0 copy-done.3
  1.3 0.0 copy-done.4
  1.4 0.0 copy-done.1
  1.4 0.0 copy-done.2
  1.4 0.0 copy-done.5
  1.4 0.0 copy-start
  1.4 1.0 %copy-done = f32[1,48,4,384]{3,2,1,0:T(4,128)S(1)} copy-done((f32[1,48,4,384]{3,2,1,0:T(4,128)S(1)}, f32[1,48,4,384]{3,2,1,0:T(4,128)}, u32[]{:S(2)}) %copy-start) | copy-done | bytes 294936
  2.4 32.7 %shard_map.119 = (f32[4,48,384]{2,1,0:T(8,128)S(1)}, f32[2,128]{1,0:T(2,128)S(1)}) custom-call(f32[48,4,384]{2,1,0:T(4,128)S(1)} %bitcast.15, f32[1,64]{1,0:T(1,128)S(1)} %bitcast.18, f32[1,64]{1,0:T(1,128)S(1)} %bitcast.19, f32[1,64]{1,0:T(1,128)S(1)} %bitcast.20, s32[2,192]{1,0:T(2,128)S(1)} %copy-done.1, s32[2,2]{1,0:T(2,128)S(1)} %bitcast.17, ...), custom_call_target="tpu_custom_call" | custom-call | tf_op jit(solution)/shard_map/pallas_call | solution.py:705
  35.0 0.8 %copy.13 = f32[1,48,4,384]{3,2,1,0:T(4,128)} copy(f32[1,48,4,384]{3,1,2,0:T(8,128)S(1)} %bitcast.16) | data formatting | bytes 589824
  35.9 0.6 %slice.12 = f32[1,1]{1,0:T(1,128)} slice(f32[2,128]{1,0:T(2,128)S(1)} %get-tuple-element.8), slice={[1:2], [64:65]} | slice | bytes 8 | tf_op jit(solution)/shard_map/slice | solution.py:767
  36.4 0.6 %slice_bitcast_fusion = (f32[64]{0:T(128)}, f32[64]{0:T(128)}, f32[64]{0:T(128)}) fusion(f32[2,128]{1,0:T(2,128)S(1)} %get-tuple-element.8), kind=kLoop, calls=%fused_computation | loop fusion | bytes 1536 | tf_op jit(solution)/shard_map/squeeze | solution.py:766
Async XLA Ops:
  0.6 0.7 %copy-start.6 = (f32[64]{0:T(128)S(1)}, f32[64]{0:T(128)}, u32[]{:S(2)}) copy-start(f32[64]{0:T(128)} %param.10) | copy-start | bytes 772
  0.6 0.7 %copy-start.7 = (f32[64]{0:T(128)S(1)}, f32[64]{0:T(128)}, u32[]{:S(2)}) copy-start(f32[64]{0:T(128)} %param.11) | copy-start | bytes 772
  0.7 0.7 %copy-start.3 = (s32[1,256]{1,0:T(1,128)S(1)}, s32[1,256]{1,0:T(1,128)}, u32[]{:S(2)}) copy-start(s32[1,256]{1,0:T(1,128)} %cells_ref.1) | copy-start | bytes 3076
  0.7 0.7 %copy-start.4 = (f32[1,256]{1,0:T(1,128)S(1)}, f32[1,256]{1,0:T(1,128)}, u32[]{:S(2)}) copy-start(f32[1,256]{1,0:T(1,128)} %heads_ref.1) | copy-start | bytes 3076
  0.7 0.7 %copy-start.1 = (s32[2,192]{1,0:T(2,128)S(1)}, s32[2,192]{1,0:T(2,128)}, u32[]{:S(2)}) copy-start(s32[2,192]{1,0:T(2,128)} %zone_ref.1) | copy-start | bytes 4612
  0.7 0.7 %copy-start.2 = (s32[1,2,2]{2,1,0:T(2,128)S(1)}, s32[1,2,2]{2,1,0:T(2,128)}, u32[]{:S(2)}) copy-start(s32[1,2,2]{2,1,0:T(2,128)} %param.13) | copy-start | bytes 52
  0.7 0.7 %copy-start.5 = (f32[64]{0:T(128)S(1)}, f32[64]{0:T(128)}, u32[]{:S(2)}) copy-start(f32[64]{0:T(128)} %param.9) | copy-start | bytes 772
  1.4 1.0 %copy-start = (f32[1,48,4,384]{3,2,1,0:T(4,128)S(1)}, f32[1,48,4,384]{3,2,1,0:T(4,128)}, u32[]{:S(2)}) copy-start(f32[1,48,4,384]{3,2,1,0:T(4,128)} %param.8) | copy-start | bytes 884740

commit v3 on v2

--- a/solution.py
+++ b/solution.py
@@ -18,6 +18,7 @@
 PAD = 8
 LINKS = 6
 DIRECT = 64
+VMEM_BYTES = 63 * 1024 * 1024
 
 
 def nt_dot(a, b):
@@ -44,15 +45,15 @@
     count,
     groups,
     events,
-    x_ref,
-    sat_ref,
-    alpha_ref,
-    n_ref,
-    zone_ref,
-    plan_ref,
-    cells_ref,
-    heads_ref,
-    out_ref,
+    x_hbm,
+    sat_hbm,
+    alpha_hbm,
+    n_hbm,
+    zone_hbm,
+    plan_hbm,
+    cells_hbm,
+    heads_hbm,
+    out_hbm,
     small_ref,
     HB,
     KB,
@@ -75,6 +76,14 @@
     SV,
     NV,
     XV,
+    OUT,
+    sat_ref,
+    alpha_ref,
+    n_ref,
+    zone_ref,
+    plan_ref,
+    cells_ref,
+    heads_ref,
     RATE,
     ACC,
     MX,
@@ -90,9 +99,24 @@
     ev_recv,
     x_sem,
 ):
-    fetch = pltpu.make_async_copy(x_ref, XV, x_sem)
-    fetch.start()
-    depth, rows, width = x_ref.shape
+    fetches = [
+        pltpu.make_async_copy(src, dst, x_sem.at[place])
+        for place, (src, dst) in enumerate(
+            (
+                (zone_hbm, zone_ref),
+                (sat_hbm, sat_ref),
+                (alpha_hbm, alpha_ref),
+                (n_hbm, n_ref),
+                (x_hbm, XV),
+                (cells_hbm, cells_ref),
+                (heads_hbm, heads_ref),
+                (plan_hbm, plan_ref),
+            )
+        )
+    ]
+    for fetch in fetches:
+        fetch.start()
+    depth, rows, width = XV.shape
     zp = OH.shape[1]
     zones = sat_ref.shape[1]
     pos = lax.axis_index("row")
@@ -109,16 +133,21 @@
     direct = total_devices <= DIRECT
     index = me_event * count + pos
 
-    def other(k):
-        at = lax.rem(index + k, total_devices)
-        return at // count, lax.rem(at, count)
+    def ring(at, size):
+        return [at] + [
+            jnp.where(at + k >= size, at + k - size, at + k) for k in range(1, size)
+        ]
+
+    row_ring, event_ring = ring(pos, count), ring(me_event, groups)
+    others = [(e, r) for r in row_ring for e in event_ring][1:]
+    row_others = [(me_event, r) for r in row_ring[1:]]
+    event_others = [(e, pos) for e in event_ring[1:]]
+
+    def place_of(device):
+        return device[0] * count + device[1]
 
     barrier = pltpu.get_barrier_semaphore()
-    if direct:
-        greeted = [other(k) for k in range(1, total_devices)]
-    else:
-        greeted = [dev(lax.rem(pos + k, count)) for k in range(1, count)]
-        greeted += [(lax.rem(me_event + k, groups), pos) for k in range(1, groups)]
+    greeted = others if direct else row_others + event_others
     for device in greeted:
         pl.semaphore_signal(barrier, 1, device_id=device, device_id_type=pl.DeviceIdType.MESH)
 
@@ -176,6 +205,8 @@
     def recv(number):
         recv_pair(number, *pairs[number])
 
+    for fetch in fetches[:4]:
+        fetch.wait()
     TAB[...] = jnp.zeros_like(TAB)
     TAB[0:1, :zones] = sat_ref[...]
     TAB[1:2, :zones] = alpha_ref[...]
@@ -203,7 +234,8 @@
             for i in range(1, rows + 1):
                 ref[step, i, 0:PAD] = jnp.zeros((PAD, width), F32)
                 ref[step, i, PAD + depth :] = jnp.zeros((PAD, width), F32)
-    fetch.wait()
+    for fetch in fetches[4:]:
+        fetch.wait()
     for i in range(rows):
         HB[0, i + 1, deep] = XV[:, i, :]
     pl.semaphore_wait(barrier, len(greeted))
@@ -295,9 +327,10 @@
         return jnp.where(i == 0, lower_open, jnp.where(i == rows, upper_open, 1.0))
 
     def level_of(step, i):
-        return jnp.where(i > 2, plan_ref[step, 1], plan_ref[step, 0]).astype(F32)
-
-    def cell(step, i):
+        levels = plan_ref[step : step + 1].astype(F32)
+        return jnp.where(i > 2, levels[:, 1:2], levels[:, 0:1])
+
+    def cell(step, i, outer=False):
         sat, alpha, n = params(i)
         m = 1.0 - 1.0 / n
         n1 = n - 1.0
@@ -319,7 +352,10 @@
             rest = 1.0 - w
             q = sat * root * rest
             KB[step, i, c.here] = q * rest
-            IC[step, i, c.bare] = v / (scale * w)
+            if step == 1 or not outer:
+                IC[step, i, c.bare] = v / (scale * w)
+            if step == 1 and outer:
+                continue
             LG[step, i, c.bare] = log_x
             LV[step, i, c.bare] = log_v
             WW[step, i, c.bare] = w
@@ -353,24 +389,13 @@
             top_rate = rate if top_rate is None else jnp.maximum(top_rate, rate)
         RATE[step] = jnp.maximum(RATE[step], top_rate)
 
-    def max_copy(step, k):
-        return pltpu.make_async_remote_copy(
-            src_ref=MX.at[step, pos],
-            dst_ref=MX.at[step, pos],
-            send_sem=max_send.at[step, k],
-            recv_sem=max_recv.at[step, pos],
-            device_id=dev(lax.rem(pos + k, count)),
-            device_id_type=pl.DeviceIdType.MESH,
-        )
-
-    def max_got(step, k):
-        src = lax.rem(pos + k, count)
+    def max_copy(step, device, src):
         return pltpu.make_async_remote_copy(
             src_ref=MX.at[step, src],
             dst_ref=MX.at[step, src],
-            send_sem=max_send.at[step, k],
+            send_sem=max_send.at[step, device[1]],
             recv_sem=max_recv.at[step, src],
-            device_id=dev(src),
+            device_id=device,
             device_id_type=pl.DeviceIdType.MESH,
         )
 
@@ -380,12 +405,12 @@
         for start_lane in range(128, width, 128):
             tile = jnp.maximum(tile, rate[:, start_lane : start_lane + 128])
         MX[step, pos] = tile
-        for k in range(1, count):
-            max_copy(step, k).start()
+        for device in row_others:
+            max_copy(step, device, pos).start()
 
     def step_size(step):
-        for k in range(1, count):
-            max_got(step, k).wait_recv()
+        for device in row_others:
+            max_copy(step, device, device[1]).wait_recv()
         top = jnp.max(MX[step], axis=0)
         return CFL / jnp.max(top, keepdims=True)
 
@@ -398,7 +423,7 @@
     over(inner, functools.partial(flow, 0))
     recv(0)
     recv(1)
-    over(halo, first_cell)
+    over(halo, lambda i: cell(0, i, True))
     over(edges, functools.partial(flow, 0))
     send_rate(0)
     start(4)
@@ -468,7 +493,7 @@
     over(own, next_cell)
     over(inner, functools.partial(flow, 1))
     recv(4)
-    over(halo, next_cell)
+    over(halo, lambda i: cell(1, i, True))
     over(edges, functools.partial(flow, 1))
     send_rate(1)
     brims = jnp.concatenate([AB[1, 1], AB[1, rows]], axis=0)
@@ -494,11 +519,14 @@
 
     def finish(i):
         head, square, pull = last_head(i)
-        out_ref[i - 1] = head
+        OUT[:, i - 1, :] = head
         LAM[1, i] = pull
         ACC[4, 0] += fold(square)
 
-    over(own, finish)
+    for i in range(1, rows + 1):
+        finish(i)
+    write = pltpu.make_async_copy(OUT, out_hbm, x_sem.at[0])
+    write.start()
     over(halo, lambda i: (last_head(i), None)[1])
 
     def slopes(step, i, grad_k_of, change_of):
@@ -613,69 +641,67 @@
         lines = [zone_sums[0:1], zone_sums[1:2], zone_sums[2:3], loss + jnp.zeros((1, zp), F32)]
     message = jnp.concatenate(lines, axis=0)
 
-    def row_copy(k, src):
+    def sum_copy(buffer, sends, recvs, device, src, dst):
         return pltpu.make_async_remote_copy(
-            src_ref=SUMR.at[src],
-            dst_ref=SUMR.at[src],
-            send_sem=sum_send.at[k],
-            recv_sem=sum_recv.at[src],
-            device_id=dev(lax.rem(pos + k, count)),
+            src_ref=buffer.at[src],
+            dst_ref=buffer.at[src],
+            send_sem=sends.at[dst],
+            recv_sem=recvs.at[src],
+            device_id=device,
             device_id_type=pl.DeviceIdType.MESH,
         )
 
-    def event_copy(k, src):
-        return pltpu.make_async_remote_copy(
-            src_ref=SUME.at[src],
-            dst_ref=SUME.at[src],
-            send_sem=ev_send.at[k],
-            recv_sem=ev_recv.at[src],
-            device_id=(lax.rem(me_event + k, groups), pos),
-            device_id_type=pl.DeviceIdType.MESH,
-        )
-
-    def all_copy(k, src):
-        return pltpu.make_async_remote_copy(
-            src_ref=SUMR.at[src],
-            dst_ref=SUMR.at[src],
-            send_sem=sum_send.at[k],
-            recv_sem=sum_recv.at[src],
-            device_id=other(k),
-            device_id_type=pl.DeviceIdType.MESH,
-        )
+    def add_up(value, buffer, sends, recvs, devices, me, place):
+        buffer[me] = value
+        for device in devices:
+            sum_copy(buffer, sends, recvs, device, me, place(device)).start()
+        for device in devices:
+            sum_copy(buffer, sends, recvs, device, place(device), place(device)).wait_recv()
+        return jnp.sum(buffer[...], axis=0)
 
     if direct:
-        SUMR[index] = message
-        for k in range(1, total_devices):
-            all_copy(k, index).start()
-        for k in range(1, total_devices):
-            all_copy(k, lax.rem(index + k, total_devices)).wait_recv()
-        small_ref[...] = jnp.sum(SUMR[...], axis=0)
+        exchanges = [(SUMR, sum_send, sum_recv, others, index, place_of)]
     else:
-        SUMR[pos] = message
-        for k in range(1, count):
-            row_copy(k, pos).start()
-        for k in range(1, count):
-            row_copy(k, lax.rem(pos + k, count)).wait_recv()
-        SUME[me_event] = jnp.sum(SUMR[...], axis=0)
-        for k in range(1, groups):
-            event_copy(k, me_event).start()
-        for k in range(1, groups):
-            event_copy(k, lax.rem(me_event + k, groups)).wait_recv()
-        small_ref[...] = jnp.sum(SUME[...], axis=0)
+        exchanges = [
+            (SUMR, sum_send, sum_recv, row_others, pos, lambda d: d[1]),
+            (SUME, ev_send, ev_recv, event_others, me_event, lambda d: d[0]),
+        ]
+    for exchange in exchanges:
+        message = add_up(message, *exchange)
+    small_ref[...] = message
+    write.wait()
 
     for number in range(LINKS):
         sent_pair(number, *pairs[number])
-    for k in range(1, count):
-        max_copy(0, k).wait_send()
-        max_copy(1, k).wait_send()
-    if direct:
-        for k in range(1, total_devices):
-            all_copy(k, index).wait_send()
+    for device in row_others:
+        max_copy(0, device, pos).wait_send()
+        max_copy(1, device, pos).wait_send()
+    for buffer, sends, recvs, devices, me, place in exchanges:
+        for device in devices:
+            sum_copy(buffer, sends, recvs, device, me, place(device)).wait_send()
+
+
+def hand_over(
+    head_hbm, small_hbm, out_hbm, loss_ref, grad_sat_ref, grad_alpha_ref, grad_n_ref, small, sem
+):
+    move = pltpu.make_async_copy(head_hbm, out_hbm, sem.at[0])
+    fetch = pltpu.make_async_copy(small_hbm, small, sem.at[1])
+    fetch.start()
+    move.start()
+    fetch.wait()
+    zones = grad_sat_ref.shape[1]
+    lines, zp = small.shape
+    grad_sat_ref[...] = small[0:1, :zones]
+    if lines == 2:
+        period = zp // 2
+        grad_alpha_ref[...] = small[0:1, period : period + zones]
+        grad_n_ref[...] = small[1:2, :zones]
+        loss_ref[...] = small[1:2, period : period + 1]
     else:
-        for k in range(1, count):
-            row_copy(k, pos).wait_send()
-        for k in range(1, groups):
-            event_copy(k, me_event).wait_send()
+        grad_alpha_ref[...] = small[1:2, :zones]
+        grad_n_ref[...] = small[2:3, :zones]
+        loss_ref[...] = small[3:4, :1]
+    move.wait()
 
 
 def local(
@@ -697,7 +723,7 @@
     lines = 2 if 2 * zones <= zp else 4
     senders = count * groups if count * groups <= DIRECT else count
     vmem = pl.BlockSpec(memory_space=pltpu.VMEM)
-    smem = pl.BlockSpec(memory_space=pltpu.SMEM)
+    hbm = pl.BlockSpec(memory_space=pltpu.HBM)
     deep = pltpu.VMEM((STEPS, rows + 2, depth + 2 * PAD, width), F32)
     full = pltpu.VMEM((STEPS, rows + 2, depth, width), F32)
     single = pltpu.VMEM((rows + 2, depth, width), F32)
@@ -705,11 +731,11 @@
     head, small = pl.pallas_call(
         functools.partial(kernel, count, groups, groups * initial_head.shape[0]),
         out_shape=(
-            jax.ShapeDtypeStruct((rows, depth, width), F32),
+            jax.ShapeDtypeStruct((depth, rows, width), F32),
             jax.ShapeDtypeStruct((lines, zp), F32),
         ),
-        in_specs=[pl.BlockSpec(memory_space=pl.ANY)] + [vmem] * 4 + [smem] + [vmem] * 2,
-        out_specs=(vmem, vmem),
+        in_specs=[hbm] * 8,
+        out_specs=(hbm, vmem),
         scratch_shapes=[
             deep,
             deep,
@@ -731,7 +757,12 @@
             pltpu.VMEM((2, 1, sensors), F32),
             pltpu.VMEM((2, 1, sensors), F32),
             pltpu.VMEM((2, 1, sensors), F32),
-            pltpu.VMEM((depth, rows, width), F32),
+            *[pltpu.VMEM((depth, rows, width), F32)] * 2,
+            *[pltpu.VMEM((1, zones), F32)] * 3,
+            pltpu.VMEM(zone_map.shape, jnp.int32),
+            pltpu.VMEM(forcing_plan.shape[1:], jnp.int32),
+            pltpu.VMEM((1, sensors), jnp.int32),
+            pltpu.VMEM((1, sensors), F32),
             pltpu.VMEM((STEPS, 8, width), F32),
             pltpu.VMEM((5, 3, 8, width), F32),
             pltpu.VMEM((STEPS, count, 8, 128), F32),
@@ -745,10 +776,10 @@
             dma((senders,)),
             dma((groups,)),
             dma((groups,)),
-            dma,
+            dma((8,)),
         ],
         compiler_params=pltpu.CompilerParams(
-            collective_id=0, has_side_effects=True, vmem_limit_bytes=48 * 1024 * 1024
+            collective_id=0, has_side_effects=True, vmem_limit_bytes=VMEM_BYTES
         ),
     )(
         initial_head[0],
@@ -760,12 +791,19 @@
         tensiometer_cells,
         tensiometer_heads,
     )
-    final = jnp.transpose(head, (1, 0, 2))[None]
-    if lines == 2:
-        half = zp // 2
-        grads = (small[0, :zones], small[0, half : half + zones], small[1, :zones])
-        return (final, small[1, half], *grads)
-    return (final, small[3, 0], small[0, :zones], small[1, :zones], small[2, :zones])
+    final, loss, grad_sat, grad_alpha, grad_n = pl.pallas_call(
+        hand_over,
+        out_shape=(
+            jax.ShapeDtypeStruct((depth, rows, width), F32),
+            jax.ShapeDtypeStruct((1, 1), F32),
+            *[jax.ShapeDtypeStruct((1, zones), F32)] * 3,
+        ),
+        in_specs=[hbm] * 2,
+        out_specs=(hbm, *[vmem] * 4),
+        scratch_shapes=[pltpu.VMEM((lines, zp), F32), dma((2,))],
+        compiler_params=pltpu.CompilerParams(vmem_limit_bytes=VMEM_BYTES),
+    )(head, small)
+    return (final[None], loss[0, 0], grad_sat[0], grad_alpha[0], grad_n[0])
 
 
 def solution(mesh):

time: 37.2 us -> 43.9 us (1.18)
  Pallas kernels: 32.7 us -> 43.1 us
  local copies, waits for them, and re-layouts: 3.66 us -> 0 us
    pallas_call x0 -> x1, Pallas kernels: none -> 10.6 us  [local(): pl.pallas_call(hand_over, out_shape=(jax.ShapeDtypeStruct((depth, rows, w...]
    unnamed x17 -> x0, local copies, waits for them, and re-layouts: 2.49 us -> none
    squeeze x1 -> x0, local copies, waits for them, and re-layouts: 0.58 us -> none  [local(): grads = (small[0, :zones], small[0, half:half + zones], small[1, :zones])]
    slice x1 -> x0, local copies, waits for them, and re-layouts: 0.58 us -> none  [local(): return (final, small[1, half], *grads)]
where the time goes in v3:
time: 43.9 us; the launch traced here: 43.7 us
  Pallas kernels  43.1 us (98%)
  between operations  0.64 us (1%)
    pallas_call x1, Pallas kernels, local(): pl.pallas_call(functools.partial(kernel, count, groups, groups * initial_...  32.5 us
    pallas_call x1, Pallas kernels, local(): pl.pallas_call(hand_over, out_shape=(jax.ShapeDtypeStruct((depth, rows, w...  10.6 us

profile of v3, /device:TPU:0, one launch (start us, length us, event | category | flops | bytes accessed | tf_op | source)
XLA Modules:
  0.0 43.7 jit_solution(9077475040440125843)
XLA Ops:
  0.6 32.5 %shard_map.119 = (f32[48,4,384]{2,1,0:T(4,128)}, f32[2,128]{1,0:T(2,128)}) custom-call(f32[48,4,384]{2,1,0:T(4,128)} %bitcast.10, f32[1,64]{1,0:T(1,128)} %bitcast.12, f32[1,64]{1,0:T(1,128)} %bitcast.13, f32[1,64]{1,0:T(1,128)} %bitcast.14, s32[2,192]{1,0:T(2,128)} %zone_hbm.1, s32[2,2]{1,0:T(2,128)} %bitcast.11, s32[1,256]{1,0:T(1,128)} %cells_hbm.1, ...), custom_call_target="tpu_custom_call" | custom-call | tf_op jit(solution)/shard_map/pallas_call | solution.py:731
  33.1 10.6 %shard_map.120 = (f32[48,4,384]{2,1,0:T(4,128)}, f32[1,1]{1,0:T(1,128)}, f32[1,64]{1,0:T(1,128)}, f32[1,64]{1,0:T(1,128)}, f32[1,64]{1,0:T(1,128)}) custom-call(f32[48,4,384]{2,1,0:T(4,128)} %get-tuple-element.12.head_hbm, f32[2,128]{1,0:T(2,128)} %get-tuple-element.13.small_hbm), custom_call_target="tpu_custom_call" | custom-call | tf_op jit(solution)/shard_map/pallas_call | solution.py:794

commit v4 on v3

--- a/solution.py
+++ b/solution.py
@@ -18,6 +18,7 @@
 PAD = 8
 LINKS = 6
 DIRECT = 64
+PARTS = 4
 VMEM_BYTES = 63 * 1024 * 1024
 
 
@@ -682,12 +683,33 @@
 
 
 def hand_over(
-    head_hbm, small_hbm, out_hbm, loss_ref, grad_sat_ref, grad_alpha_ref, grad_n_ref, small, sem
+    head_hbm,
+    small_hbm,
+    out_hbm,
+    loss_ref,
+    grad_sat_ref,
+    grad_alpha_ref,
+    grad_n_ref,
+    head,
+    small,
+    sem,
 ):
-    move = pltpu.make_async_copy(head_hbm, out_hbm, sem.at[0])
-    fetch = pltpu.make_async_copy(small_hbm, small, sem.at[1])
+    fetch = pltpu.make_async_copy(small_hbm, small, sem.at[0, PARTS])
+    size = head.shape[0] // PARTS
+    spans = [pl.ds(part * size, size) for part in range(PARTS)]
+    moves = [
+        (
+            pltpu.make_async_copy(head_hbm.at[span], head.at[span], sem.at[0, part]),
+            pltpu.make_async_copy(head.at[span], out_hbm.at[span], sem.at[1, part]),
+        )
+        for part, span in enumerate(spans)
+    ]
+    for inward, _ in moves:
+        inward.start()
     fetch.start()
-    move.start()
+    for inward, outward in moves:
+        inward.wait()
+        outward.start()
     fetch.wait()
     zones = grad_sat_ref.shape[1]
     lines, zp = small.shape
@@ -701,7 +723,8 @@
         grad_alpha_ref[...] = small[1:2, :zones]
         grad_n_ref[...] = small[2:3, :zones]
         loss_ref[...] = small[3:4, :1]
-    move.wait()
+    for _, outward in moves:
+        outward.wait()
 
 
 def local(
@@ -800,7 +823,11 @@
         ),
         in_specs=[hbm] * 2,
         out_specs=(hbm, *[vmem] * 4),
-        scratch_shapes=[pltpu.VMEM((lines, zp), F32), dma((2,))],
+        scratch_shapes=[
+            pltpu.VMEM((depth, rows, width), F32),
+            pltpu.VMEM((lines, zp), F32),
+            dma((2, PARTS + 1)),
+        ],
         compiler_params=pltpu.CompilerParams(vmem_limit_bytes=VMEM_BYTES),
     )(head, small)
     return (final[None], loss[0, 0], grad_sat[0], grad_alpha[0], grad_n[0])

time: 43.9 us -> 35.6 us (0.81)
  Pallas kernels: 43.1 us -> 34.7 us
    pallas_call x1, Pallas kernels: 10.6 us -> 2.24 us  [local(): pl.pallas_call(hand_over, out_shape=(jax.ShapeDtypeStruct((depth, rows, w...]
where the time goes in v4:
time: 35.6 us; the launch traced here: 35.4 us
  Pallas kernels  34.7 us (97%)
  between operations  0.64 us (2%)
    pallas_call x1, Pallas kernels, local(): pl.pallas_call(functools.partial(kernel, count, groups, groups * initial_...  32.5 us
    pallas_call x1, Pallas kernels, local(): pl.pallas_call(hand_over, out_shape=(jax.ShapeDtypeStruct((depth, rows, w...  2.24 us

profile of v4, /device:TPU:0, one launch (start us, length us, event | category | flops | bytes accessed | tf_op | source)
XLA Modules:
  0.0 35.4 jit_solution(77738594812687777)
XLA Ops:
  0.6 32.5 %shard_map.119 = (f32[48,4,384]{2,1,0:T(4,128)}, f32[2,128]{1,0:T(2,128)}) custom-call(f32[48,4,384]{2,1,0:T(4,128)} %bitcast.10, f32[1,64]{1,0:T(1,128)} %bitcast.12, f32[1,64]{1,0:T(1,128)} %bitcast.13, f32[1,64]{1,0:T(1,128)} %bitcast.14, s32[2,192]{1,0:T(2,128)} %zone_hbm.1, s32[2,2]{1,0:T(2,128)} %bitcast.11, s32[1,256]{1,0:T(1,128)} %cells_hbm.1, ...), custom_call_target="tpu_custom_call" | custom-call | tf_op jit(solution)/shard_map/pallas_call | solution.py:754
  33.1 2.2 %shard_map.120 = (f32[48,4,384]{2,1,0:T(4,128)}, f32[1,1]{1,0:T(1,128)}, f32[1,64]{1,0:T(1,128)}, f32[1,64]{1,0:T(1,128)}, f32[1,64]{1,0:T(1,128)}) custom-call(f32[48,4,384]{2,1,0:T(4,128)} %get-tuple-element.12.head_hbm, f32[2,128]{1,0:T(2,128)} %get-tuple-element.13.small_hbm), custom_call_target="tpu_custom_call" | custom-call | tf_op jit(solution)/shard_map/pallas_call | solution.py:817

commit v5 on v4

--- a/solution.py
+++ b/solution.py
@@ -104,11 +104,11 @@
         pltpu.make_async_copy(src, dst, x_sem.at[place])
         for place, (src, dst) in enumerate(
             (
+                (x_hbm, XV),
                 (zone_hbm, zone_ref),
                 (sat_hbm, sat_ref),
                 (alpha_hbm, alpha_ref),
                 (n_hbm, n_ref),
-                (x_hbm, XV),
                 (cells_hbm, cells_ref),
                 (heads_hbm, heads_ref),
                 (plan_hbm, plan_ref),
@@ -206,8 +206,15 @@
     def recv(number):
         recv_pair(number, *pairs[number])
 
-    for fetch in fetches[:4]:
+    fetches[0].wait()
+    for i in (0, rows - 1):
+        HB[0, i + 1, deep] = XV[:, i, :]
+    pl.semaphore_wait(barrier, len(greeted))
+    start(0)
+    for fetch in fetches[1:]:
         fetch.wait()
+    start(2)
+    start(3)
     TAB[...] = jnp.zeros_like(TAB)
     TAB[0:1, :zones] = sat_ref[...]
     TAB[1:2, :zones] = alpha_ref[...]
@@ -230,20 +237,14 @@
         OH[pair + 1] = jnp.where(zone_of == own_ids, 1.0, 0.0).astype(BF16)
         block = three(TAB[...], lambda t: jnp.dot(t, OH[pair + 1], preferred_element_type=F32))
         PB[pair + 1] = jnp.where(part_line == 3, own_ids, block)
+    start(1)
     for ref in (HB, KB, GB):
         for step in range(STEPS):
             for i in range(1, rows + 1):
                 ref[step, i, 0:PAD] = jnp.zeros((PAD, width), F32)
                 ref[step, i, PAD + depth :] = jnp.zeros((PAD, width), F32)
-    for fetch in fetches[4:]:
-        fetch.wait()
-    for i in range(rows):
+    for i in range(1, rows - 1):
         HB[0, i + 1, deep] = XV[:, i, :]
-    pl.semaphore_wait(barrier, len(greeted))
-    start(0)
-    start(1)
-    start(2)
-    start(3)
 
     @pl.when(jnp.logical_not(has_up))
     def _():

time: 35.6 us -> 35.6 us (level)
  no operation moved by 1% of the time
where the time goes in v5:
time: 35.6 us; the launch traced here: 35.4 us
  Pallas kernels  34.8 us (98%)
  between operations  0.64 us (2%)
    pallas_call x1, Pallas kernels, local(): pl.pallas_call(functools.partial(kernel, count, groups, groups * initial_...  32.5 us
    pallas_call x1, Pallas kernels, local(): pl.pallas_call(hand_over, out_shape=(jax.ShapeDtypeStruct((depth, rows, w...  2.24 us

profile of v5, /device:TPU:0, one launch (start us, length us, event | category | flops | bytes accessed | tf_op | source)
XLA Modules:
  0.0 35.4 jit_solution(6150693981780023385)
XLA Ops:
  0.6 32.5 %shard_map.119 = (f32[48,4,384]{2,1,0:T(4,128)}, f32[2,128]{1,0:T(2,128)}) custom-call(f32[48,4,384]{2,1,0:T(4,128)} %bitcast.10, f32[1,64]{1,0:T(1,128)} %bitcast.12, f32[1,64]{1,0:T(1,128)} %bitcast.13, f32[1,64]{1,0:T(1,128)} %bitcast.14, s32[2,192]{1,0:T(2,128)} %zone_hbm.1, s32[2,2]{1,0:T(2,128)} %bitcast.11, s32[1,256]{1,0:T(1,128)} %cells_hbm.1, ...), custom_call_target="tpu_custom_call" | custom-call | tf_op jit(solution)/shard_map/pallas_call | solution.py:755
  33.2 2.2 %shard_map.120 = (f32[48,4,384]{2,1,0:T(4,128)}, f32[1,1]{1,0:T(1,128)}, f32[1,64]{1,0:T(1,128)}, f32[1,64]{1,0:T(1,128)}, f32[1,64]{1,0:T(1,128)}) custom-call(f32[48,4,384]{2,1,0:T(4,128)} %get-tuple-element.12.head_hbm, f32[2,128]{1,0:T(2,128)} %get-tuple-element.13.small_hbm), custom_call_target="tpu_custom_call" | custom-call | tf_op jit(solution)/shard_map/pallas_call | solution.py:818

commit v6 on v5

--- a/solution.py
+++ b/solution.py
@@ -17,7 +17,7 @@
 LAYERS = 16
 PAD = 8
 LINKS = 6
-DIRECT = 64
+DIRECT = 16
 PARTS = 4
 VMEM_BYTES = 63 * 1024 * 1024
 

time: 35.6 us -> 36.4 us (1.022)
  Pallas kernels: 34.8 us -> 35.6 us
    pallas_call x1, Pallas kernels: 32.5 us -> 33.3 us  [local(): pl.pallas_call(functools.partial(kernel, count, groups, groups * initial_...]
where the time goes in v6:
time: 36.4 us; the launch traced here: 36.2 us
  Pallas kernels  35.6 us (98%)
  between operations  0.64 us (2%)
    pallas_call x1, Pallas kernels, local(): pl.pallas_call(functools.partial(kernel, count, groups, groups * initial_...  33.3 us
    pallas_call x1, Pallas kernels, local(): pl.pallas_call(hand_over, out_shape=(jax.ShapeDtypeStruct((depth, rows, w...  2.24 us

profile of v6, /device:TPU:0, one launch (start us, length us, event | category | flops | bytes accessed | tf_op | source)
XLA Modules:
  0.0 36.2 jit_solution(5359100638257332861)
XLA Ops:
  0.6 33.3 %shard_map.119 = (f32[48,4,384]{2,1,0:T(4,128)}, f32[2,128]{1,0:T(2,128)}) custom-call(f32[48,4,384]{2,1,0:T(4,128)} %bitcast.10, f32[1,64]{1,0:T(1,128)} %bitcast.12, f32[1,64]{1,0:T(1,128)} %bitcast.13, f32[1,64]{1,0:T(1,128)} %bitcast.14, s32[2,192]{1,0:T(2,128)} %zone_hbm.1, s32[2,2]{1,0:T(2,128)} %bitcast.11, s32[1,256]{1,0:T(1,128)} %cells_hbm.1, ...), custom_call_target="tpu_custom_call" | custom-call | tf_op jit(solution)/shard_map/pallas_call | solution.py:755
  34.0 2.2 %shard_map.120 = (f32[48,4,384]{2,1,0:T(4,128)}, f32[1,1]{1,0:T(1,128)}, f32[1,64]{1,0:T(1,128)}, f32[1,64]{1,0:T(1,128)}, f32[1,64]{1,0:T(1,128)}) custom-call(f32[48,4,384]{2,1,0:T(4,128)} %get-tuple-element.12.head_hbm, f32[2,128]{1,0:T(2,128)} %get-tuple-element.13.small_hbm), custom_call_target="tpu_custom_call" | custom-call | tf_op jit(solution)/shard_map/pallas_call | solution.py:818
